TPU v7x, 512 devices: a whole 4x8x8 slice. The times are simulated.
512 devices in a mesh: lat: 32 (over x_hi, y, core), lon: 16 (over z, x_lo).
Axes of the slice: x: 4 (x_hi: 2, x_lo: 2; x = x_hi * 2 + x_lo), y: 8, z: 8, core: 2. Of those that a mesh axis runs over, the one named last changes fastest.
Arguments:
- flow_state: float32 [5, 9, 4, 512, 2048], P(None, None, None, 'lat', 'lon'), may hold values from -8 to 8
- jacobian_lat: float32 [5, 5], replicated, may hold values from -2.5 to 2.5
- jacobian_lon: float32 [5, 5], replicated, may hold values from -2.5 to 2.5
- jacobian_rad: float32 [5, 5], replicated, may hold values from -2.5 to 2.5
- ratio_real: float32 [256, 5], replicated, may hold values from -1.5 to -0.3
- ratio_imag: float32 [256, 4], replicated, may hold values from -1 to 1
- degree_cut: int32 [5], replicated, may hold values from 128 to 255, as said below
Outputs:
- residual: float32 [5, 9, 4, 512, 2048], P(None, None, None, 'lat', 'lon')
- normal_derivative: float32 [5, 9, 512, 2048], P(None, None, 'lat', 'lon')
Inputs may be any that keep to these rules, and one draw needn't show every extreme that they name: degree_cut[n] is the highest degree kept at time frequency n.
All inputs are finite; a program needn't handle non-finite values.
Results may differ from a plain program's by a relative error of at most 0.001.
Values sent between devices are 32-bit elements; how exact they have to be, the bound alone decides.
A program may use at most 128 MiB of HBM per device.

v0:
```python
import math

import jax
import jax.numpy as jnp
from jax import lax
from jax.sharding import PartitionSpec as P

M_DEV = 16


damping = 0.5
highest = lax.Precision.HIGHEST
start_floor = -36.0


def extended(cells, sides, width):
    for axis, dim in sides:
        count = lax.axis_size(axis)
        head = lax.slice_in_dim(cells, 0, width, axis=dim)
        tail = lax.slice_in_dim(cells, cells.shape[dim] - width, cells.shape[dim], axis=dim)
        cells = jnp.concatenate(
            [
                lax.ppermute(tail, axis, [(i, (i + 1) % count) for i in range(count)]),
                cells,
                lax.ppermute(head, axis, [((i + 1) % count, i) for i in range(count)]),
            ],
            axis=dim,
        )
    return cells


def fejer_weights(lat_index, total_rows):
    series_terms = jnp.arange(1, total_rows // 2 + 1, dtype=jnp.int32)
    phase_index = series_terms[None, :] * (2 * lat_index[:, None] + 1) % (2 * total_rows)
    angles = phase_index.astype(jnp.float32) * (math.pi / total_rows)
    divisor = (4 * series_terms * series_terms - 1).astype(jnp.float32)
    series = jnp.sum(jnp.cos(angles) / divisor[None, :], axis=1)
    return 2.0 / total_rows * (1.0 - 2.0 * series)


def legendre_matrix(orders, colatitude, harmonic_degree_total):
    cosine = jnp.cos(colatitude)[None, :]
    order_f = orders.astype(jnp.float32)[:, None]
    log_start = 0.5 * (
        jnp.log((2.0 * order_f + 1.0) / (4.0 * math.pi))
        + lax.lgamma(order_f + 0.5)
        - lax.lgamma(order_f + 1.0)
        - 0.5 * math.log(math.pi)
    )
    log_diagonal = log_start + order_f * jnp.log(jnp.sin(colatitude))[None, :]
    diagonal = jnp.where(
        log_diagonal >= start_floor, jnp.exp(jnp.maximum(log_diagonal, start_floor)), 0.0
    )

    def advance(state_pair, degree):
        latest, before = state_pair
        degree_f = degree.astype(jnp.float32)
        factor = jnp.sqrt(
            jnp.maximum(4.0 * degree_f * degree_f - 1.0, 1.0)
            / jnp.maximum(degree_f * degree_f - order_f * order_f, 1.0)
        )
        degree_prev = degree_f - 1.0
        factor_prev = jnp.sqrt(
            jnp.maximum(4.0 * degree_prev * degree_prev - 1.0, 1.0)
            / jnp.maximum(degree_prev * degree_prev - order_f * order_f, 1.0)
        )
        quotient = jnp.where(degree_prev > order_f, factor / factor_prev, 0.0)
        grown = factor * cosine * latest - quotient * before
        fresh_row = jnp.where(
            degree_f == order_f, diagonal, jnp.where(degree_f > order_f, grown, 0.0)
        )
        return ((fresh_row, latest), fresh_row)

    zero_rows = jnp.zeros_like(diagonal)
    _, legendre = lax.scan(
        advance,
        (zero_rows, zero_rows),
        jnp.arange(harmonic_degree_total, dtype=jnp.int32),
        unroll=16,
    )
    return legendre


def instance_kernel(ratio_real, ratio_imag, degree_cut, first_degree, amount):
    sample_moment_number = 2 * ratio_imag.shape[1] + 1
    degree = first_degree + jnp.arange(amount, dtype=jnp.int32)
    keep = (degree[:, None] <= degree_cut[None, :]).astype(jnp.float32)
    real_part = lax.dynamic_slice_in_dim(ratio_real, first_degree, amount, 0) * keep
    imag_part = lax.dynamic_slice_in_dim(ratio_imag, first_degree, amount, 0) * keep[:, 1:]
    period_sample_points = jnp.arange(sample_moment_number, dtype=jnp.int32)
    moment_shift_lag = period_sample_points[:, None] - period_sample_points[None, :]
    harmonic = jnp.arange(1, ratio_real.shape[1], dtype=jnp.int32)
    phase_index = harmonic[:, None, None] * moment_shift_lag[None] % sample_moment_number
    angles = phase_index.astype(jnp.float32) * (2.0 * math.pi / sample_moment_number)
    kernel = (
        real_part[:, :1, None]
        + 2.0 * jnp.einsum("ln,nts->lts", real_part[:, 1:], jnp.cos(angles), precision=highest)
        - 2.0 * jnp.einsum("ln,nts->lts", imag_part, jnp.sin(angles), precision=highest)
    )
    return kernel / sample_moment_number


def spectral_matrix(sample_moment_number):
    period_sample_points = jnp.arange(sample_moment_number, dtype=jnp.int32)
    moment_shift_lag = period_sample_points[:, None] - period_sample_points[None, :]
    parity = jnp.where(moment_shift_lag % 2 == 0, 1.0, -1.0).astype(jnp.float32)
    safe_lag = jnp.where(moment_shift_lag == 0, 1, moment_shift_lag).astype(jnp.float32)
    return jnp.where(
        moment_shift_lag == 0,
        0.0,
        0.5 * parity / jnp.sin(math.pi * safe_lag / sample_moment_number),
    )


def mix_vars(matrix, difference):
    return jnp.einsum("vw,w...->v...", matrix, difference, precision=highest)


def layer_residual(
    centre,
    inner_layer,
    outer_layer,
    north_row,
    south_row,
    west_col,
    east_col,
    sine_lat,
    jacobian_lat,
    jacobian_lon,
    jacobian_rad,
):
    flux_sum = sine_lat * (
        mix_vars(jacobian_lat, 0.5 * (south_row - north_row))
        + mix_vars(jacobian_rad, 0.5 * (outer_layer - inner_layer))
    ) + mix_vars(jacobian_lon, 0.5 * (east_col - west_col))
    spread = sine_lat * (south_row + north_row + outer_layer + inner_layer - 4.0 * centre) + (
        east_col + west_col - 2.0 * centre
    )
    timing = jnp.einsum(
        "ts,vs...->vt...", spectral_matrix(centre.shape[1]), centre, precision=highest
    )
    return timing + flux_sum - damping * spread


def column_orders(columns, per_device):
    device = columns // (2 * per_device)
    component = columns // per_device % 2
    azimuth_order_index = device * per_device + columns % per_device
    return (component, azimuth_order_index)


def forward_table(columns, positions, per_device, total_cols):
    component, azimuth_order_index = column_orders(columns, per_device)
    angles = (positions[:, None] * azimuth_order_index[None, :] % total_cols).astype(
        jnp.float32
    ) * (2.0 * math.pi / total_cols)
    return jnp.where(component[None, :] == 0, jnp.cos(angles), -jnp.sin(angles)) * (
        2.0 * math.pi / total_cols
    )


def inverse_table(columns, positions, per_device, total_cols):
    component, azimuth_order_index = column_orders(columns, per_device)
    angles = (azimuth_order_index[:, None] * positions[None, :] % total_cols).astype(
        jnp.float32
    ) * (2.0 * math.pi / total_cols)
    order_weight = jnp.where(azimuth_order_index == 0, 1.0, 2.0)[:, None]
    return jnp.where(component[:, None] == 0, jnp.cos(angles), -jnp.sin(angles)) * order_weight


def regroup(block_rows, convert):
    return lax.all_to_all(
        convert(lax.all_to_all(block_rows, "lon", split_axis=0, concat_axis=2, tiled=True)),
        "lon",
        split_axis=2,
        concat_axis=0,
        tiled=True,
    )


def shards(
    flow_state, jacobian_lat, jacobian_lon, jacobian_rad, ratio_real, ratio_imag, degree_cut
):
    num_vars, sample_moment_number, num_rad, lat_rows, lon_cols = flow_state.shape
    fields = num_vars * sample_moment_number
    lat_count = lax.axis_size("lat")
    lon_count = lax.axis_size("lon")
    total_lat = lat_rows * lat_count
    total_lon = lon_cols * lon_count
    mode_count = M_DEV * lon_count
    degree_rows = mode_count // lat_count
    lat_index = lax.axis_index("lat") * lat_rows + jnp.arange(lat_rows, dtype=jnp.int32)
    colatitude = (lat_index.astype(jnp.float32) + 0.5) * (math.pi / total_lat)
    weights = fejer_weights(lat_index, total_lat)
    orders = lax.axis_index("lon") * M_DEV + jnp.arange(M_DEV, dtype=jnp.int32)
    farfield_shell = jnp.transpose(
        flow_state[:, :, num_rad - 1].reshape(fields, lat_rows, lon_cols), (1, 0, 2)
    )

    def analyse_lon(gathered):
        fourier_basis = forward_table(
            jnp.arange(2 * mode_count, dtype=jnp.int32),
            jnp.arange(total_lon, dtype=jnp.int32),
            M_DEV,
            total_lon,
        )
        return jnp.einsum("jfk,kc->jfc", gathered, fourier_basis, precision=highest)

    fourier = regroup(farfield_shell, analyse_lon)
    fourier = fourier.reshape(lat_rows, fields, 2, M_DEV) * weights[:, None, None, None]
    legendre = legendre_matrix(orders, colatitude, mode_count)
    table_rows = legendre
    coef_block = jnp.einsum("lmj,jfcm->lmfc", table_rows, fourier, precision=highest)
    coefficients = lax.psum_scatter(
        coef_block.reshape(degree_rows * lax.axis_size("lat"), M_DEV * fields * 2),
        "lat",
        scatter_dimension=0,
        tiled=True,
    )
    kernel = instance_kernel(
        ratio_real, ratio_imag, degree_cut, lax.axis_index("lat") * degree_rows, degree_rows
    )
    shaped = coefficients.reshape(degree_rows, M_DEV, num_vars, sample_moment_number, 2)
    bent_coef = jnp.einsum("lts,lmvsc->lmvtc", kernel, shaped, precision=highest).reshape(
        degree_rows, M_DEV * fields * 2
    )
    portion = lax.all_gather(bent_coef, "lat", axis=0, tiled=True)
    amount = portion.shape[0]
    table_rows = legendre
    synthesised = jnp.einsum(
        "lmj,lmfc->jfcm", table_rows, portion.reshape(amount, M_DEV, fields, 2), precision=highest
    )
    synthesised = synthesised.reshape(lat_rows, fields, 2 * M_DEV)

    def synthesise_lon(gathered):
        order_basis = inverse_table(
            jnp.arange(2 * mode_count, dtype=jnp.int32),
            jnp.arange(total_lon, dtype=jnp.int32),
            M_DEV,
            total_lon,
        )
        return jnp.einsum("jfc,ck->jfk", gathered, order_basis, precision=highest)

    normal = regroup(synthesised, synthesise_lon)
    normal = jnp.transpose(normal, (1, 0, 2)).reshape(
        num_vars, sample_moment_number, lat_rows, lon_cols
    )
    padded = extended(flow_state, (("lat", 3), ("lon", 4)), 1)
    border_latitude_lines = jnp.arange(lat_rows + 2, dtype=jnp.int32)
    at_pole = (border_latitude_lines == 0) & (lax.axis_index("lat") == 0) | (
        border_latitude_lines == lat_rows + 1
    ) & (lax.axis_index("lat") == lat_count - 1)
    padded = jnp.where(at_pole[:, None], 0.0, padded)
    north_row = padded[:, :, :, :-2, 1:-1]
    south_row = padded[:, :, :, 2:, 1:-1]
    west_col = padded[:, :, :, 1:-1, :-2]
    east_col = padded[:, :, :, 1:-1, 2:]
    ghost_layer = flow_state[:, :, num_rad - 1] + normal
    empty_layer = jnp.zeros_like(flow_state[:, :, :1])
    inner_layer = jnp.concatenate([empty_layer, flow_state[:, :, :-1]], axis=2)
    outer_layer = jnp.concatenate([flow_state[:, :, 1:], ghost_layer[:, :, None]], axis=2)
    sine_lat = jnp.sin(colatitude)[:, None]
    residual = layer_residual(
        flow_state,
        inner_layer,
        outer_layer,
        north_row,
        south_row,
        west_col,
        east_col,
        sine_lat,
        jacobian_lat,
        jacobian_lon,
        jacobian_rad,
    )
    return (residual, normal)


def solution(mesh):
    placed = (P(None, None, None, "lat", "lon"), P(), P(), P(), P(), P(), P())
    return jax.shard_map(
        shards,
        mesh=mesh,
        in_specs=placed,
        out_specs=(P(None, None, None, "lat", "lon"), P(None, None, "lat", "lon")),
        check_vma=False,
    )
```

profile of v0, /device:TPU:1, one launch (start us, length us, event | category | flops | bytes accessed | tf_op | source)
XLA Modules:
  0.0 609.4 jit_solution(9994572024874302679)
XLA Ops:
  9.1 11.9 %all-to-all-start = ((f32[16,45,128]{2,1,0:T(8,128)}), f32[16,45,128]{2,1,0:T(8,128)S(1)}, u32[]{:S(2)}, u32[]{:S(2)}) async-start(f32[16,45,128]{2,1,0:T(8,128)} %copy.190), calls=%async_computation | async-start | bytes 786432 | tf_op jit(solution)/shard_map/all_to_all | solution.py:173
  21.2 209.1 %while.20 = (s32[]{:T(128)}, f32[16,16]{1,0:T(8,128)S(1)}, f32[16,16]{1,0:T(8,128)S(1)}, f32[16,16,16,16]{3,2,1,0:T(8,128)S(1)}, s32[16,16]{1,0:T(8,128)S(1)}, /...) while((s32[]{:T(128)}, f32[16,16]{1,0:T(8,128)S(1)}, ...), condition=%wide.region_2.3_spmd.clone.clone.clone, body=%wide.region_1.2_spmd.clone.clone.clone.sunk | while | flops 74626 | bytes 854063 | solution.py:75
  230.3 1.1 copy.221
  232.0 19.7 %fusion.88 = f32[1,45,512]{2,1,0:T(8,128)S(1)} fusion(f32[45,2048]{1,0:T(8,128)S(1)} %bitcast.510, s32[512]{0:T(512)S(1)} %fusion.146, pred[512]{0:T(512)(128)(4,1)S(1)} %fusion.143), kind=kOutput, calls=%fused_computation.200 | convolution fusion | flops 584056832 | bytes 463360 | tf_op jit(solution)/shard_map/jfk,kc->jfc/dot_general | solution.py:207
  252.3 1.2 reduce
  254.6 7.5 %all-to-all-start.1 = ((f32[16,1,1440]{2,1,0:T(1,128)}), f32[16,1,1440]{2,1,0:T(1,128)S(1)}, u32[]{:S(2)}, u32[]{:S(2)}) async-start(f32[16,1,1440]{2,1,0:T(1,128)} %reshape.1746), calls=%async_computation.1 | async-start | bytes 196608 | tf_op jit(solution)/shard_map/all_to_all | solution.py:172
  262.4 7.9 %all-to-all-done.1 = f32[16,1,1440]{2,1,0:T(1,128)S(1)} async-done(((f32[16,1,1440]{2,1,0:T(1,128)}), f32[16,1,1440]{2,1,0:T(1,128)S(1)}, u32[]{:S(2)}, u32[]{:S(2)}) %all-to-all-start.1) | async-done | bytes 92192 | tf_op jit(solution)/shard_map/all_to_all | solution.py:172
  272.2 1.5 convolution_bitcast_fusion
  273.8 1.1 copy.197
  276.0 1.6 copy.234
  278.7 117.4 %reduce-scatter.4.cloned.1.call-done = f32[8,1440]{1,0:T(8,128)} async-done(((f32[256,1440]{1,0:T(8,128)}), f32[8,1440]{1,0:T(8,128)}) %reduce-scatter.4.cloned.1.call-update) | async-done | bytes 46096
  396.1 1.1 copy.235
  397.1 1.1 copy.198
  399.0 1.2 copy.200
  401.3 7.8 %collective-permute-start = (f32[5,9,4,1,128]{4,3,0,2,1:T(1,128)S(1)}, f32[5,9,4,1,128]{4,3,0,2,1:T(1,128)S(1)}, u32[]{:S(2)}, u32[]{:S(2)}) collective-permute-start(f32[5,9,4,1,128]{4,3,0,2,1:T(1,128)S(1)} %get-tuple-element.470), channel_id=1, source_target_pairs={{0,16},{16,32},{32,48},{48,64},{64,80},{80,96},{96,112},{112,128},... | collective-permute-start | bytes 276488 | tf_op jit(solution)/shard_map/ppermute | solution.py:23
  409.1 2.3 collective-permute-start.1
  411.5 1.2 fusion.201
  412.7 4.5 fusion.55
  417.5 2.8 fusion.200
  420.4 2.8 copy.182
  423.2 2.8 copy.183
  426.0 5.7 collective-permute-start.3
  431.7 1.9 collective-permute-start.2
  433.6 5.5 collective-permute-done.2
  439.1 2.5 copy.184
  441.6 2.6 copy.185
  444.3 45.0 %all-gather.2.cloned.1.call-done = f32[256,1440]{1,0:T(8,128)} async-done(((f32[8,1440]{1,0:T(8,128)}), f32[256,1440]{1,0:T(8,128)}) %all-gather.2.cloned.1.call-update) | async-done | bytes 1474576 | tf_op jit(solution)/shard_map/all_gather | solution.py:227
  489.3 3.0 copy.202
  492.3 3.0 reshape.1727
  495.3 3.7 fusion.85
  499.2 1.0 reshape.1748
  500.2 7.2 %all-to-all-start.2 = ((f32[16,1,1440]{2,1,0:T(1,128)}), f32[16,1,1440]{2,1,0:T(1,128)S(1)}, u32[]{:S(2)}, u32[]{:S(2)}) async-start(f32[16,1,1440]{2,1,0:T(1,128)} %reshape.1748), calls=%async_computation.2 | async-start | bytes 196608 | tf_op jit(solution)/shard_map/all_to_all | solution.py:173
  507.4 6.3 %maximum_select_fusion = f32[5,9,4,18,130]{4,3,0,2,1:T(8,128)} fusion(f32[5,9,4,18,1]{4,3,0,2,1:T(8,128)} %copy.185, f32[5,9,4,1,128]{4,3,0,2,1:T(1,128)S(1)} %collective-permute-done.1, f32[5,9,4,1,128]{4,3,0,2,1:T(1,128)S(1)} %collective-permute-done, f32[5,9,4,18,1]{4,3,0,2,1:T(8,128)} %copy.184, pred[18]{0:T(512)(128)(4,1)S(1)} %and_or_fusion, ...), kind=kLoop, calls=%fused_computation.133 | loop fusion | flops 2106000 | bytes 3369618 | tf_op jit(solution)/shard_map/jit(_where)/select_n | solution.py:253
  513.7 1.9 all-to-all-done.2
  516.7 24.1 %fusion.33 = f32[45,2048]{0,1:T(8,128)} fusion(f32[45,512]{0,1:T(8,128)S(1)} %bitcast.511, f32[512]{0:T(512)S(1)} %compare_select_fusion.4, s32[512]{0:T(512)S(1)} %fusion.146, pred[512]{0:T(512)(128)(4,1)S(1)} %fusion.143), kind=kOutput, calls=%fused_computation.140 | convolution fusion | flops 584056832 | bytes 465408 | tf_op jit(solution)/shard_map/jfc,ck->jfk/dot_general | solution.py:242
  540.8 11.6 %reduce.3 = f32[2048,45]{1,0:T(8,128)} reduce(f32[2048,1,45]{2,1,0:T(1,128)} %bitcast.505, f32[]{:T(128)} %broadcast.3172), dimensions={1}, to_apply=%bitcast.338.reduce_sub_computation | reduce | bytes 737284
  552.4 3.1 reshape.1750
  555.5 5.7 all-to-all-start.3
  561.2 6.4 %subtract_multiply_fusion.1 = (f32[5,9,4,16,128]{4,3,0,2,1:T(8,128)S(1)}, f32[5,9,4,16,128]{4,3,0,2,1:T(8,128)S(1)}) fusion(f32[5,9,4,18,130]{4,3,0,2,1:T(8,128)} %maximum_select_fusion), kind=kLoop, calls=%fused_computation.197 | loop fusion | flops 1474560 | bytes 8847360 | tf_op jit(solution)/shard_map/mul | solution.py:133
  567.6 3.9 fusion.61
  571.6 4.0 fusion.57
  575.6 1.4 reduce.4
  577.0 3.0 reshape.1751
  580.0 2.6 copy.208
  582.7 1.3 copy-done.2
  584.7 4.0 fusion.59
  588.7 10.9 %fusion.83 = f32[5,9,4,16,128]{4,3,0,2,1:T(8,128)} fusion(f32[5,9,3,16,128]{4,3,0,2,1:T(8,128)} %get-tuple-element.469, f32[9,4,16,128,5]{3,4,2,1,0:T(8,128)} %fusion.57, f32[9,4,16,128,5]{3,4,2,1,0:T(8,128)} %fusion.59, f32[9,4,16,128,5]{3,4,2,1,0:T(8,128)} %fusion.61, f32[9,5,4,16,128]{4,0,3,2,1:T(8,128)} %fusion.55, ...), kind=kLoop, calls=%fused_computation.190 | loop fusion | flops 6266880 | bytes 17327104 | tf_op jit(solution)/shard_map/sub | solution.py:142
  599.6 2.7 copy.218
  (778 shorter events, 54.4 us)
Async XLA Ops:
  7.2 560.4 %copy-start = (f32[5,5]{1,0:T(8,128)S(1)}, f32[5,5]{1,0:T(8,128)}, u32[]{:S(2)}) copy-start(f32[5,5]{1,0:T(8,128)} %param.10) | copy-start | bytes 304
  9.1 222.5 %all-to-all-start = ((f32[16,45,128]{2,1,0:T(8,128)}), f32[16,45,128]{2,1,0:T(8,128)S(1)}, u32[]{:S(2)}, u32[]{:S(2)}) async-start(f32[16,45,128]{2,1,0:T(8,128)} %copy.190), calls=%async_computation | async-start | bytes 786432 | tf_op jit(solution)/shard_map/all_to_all | solution.py:173
  254.6 15.7 %all-to-all-start.1 = ((f32[16,1,1440]{2,1,0:T(1,128)}), f32[16,1,1440]{2,1,0:T(1,128)S(1)}, u32[]{:S(2)}, u32[]{:S(2)}) async-start(f32[16,1,1440]{2,1,0:T(1,128)} %reshape.1746), calls=%async_computation.1 | async-start | bytes 196608 | tf_op jit(solution)/shard_map/all_to_all | solution.py:172
  262.1 133.9 %reduce-scatter.4.cloned.1.call-start = ((), (), s32[]{:S(2)}) async-start(), calls=%async_computation.6 | async-start | bytes 1622016
  275.9 1.8 copy-start.7
  275.9 1.9 copy-start.6
  277.6 0.7 copy-start.8
  277.6 211.7 %all-gather.2.cloned.1.call-start = ((), (), s32[]{:S(2)}) async-start(), calls=%async_computation.5 | async-start | bytes 1622016 | tf_op jit(solution)/shard_map/all_gather | solution.py:227
  398.3 2.8 copy-start.1
  401.3 15.9 %collective-permute-start = (f32[5,9,4,1,128]{4,3,0,2,1:T(1,128)S(1)}, f32[5,9,4,1,128]{4,3,0,2,1:T(1,128)S(1)}, u32[]{:S(2)}, u32[]{:S(2)}) collective-permute-start(f32[5,9,4,1,128]{4,3,0,2,1:T(1,128)S(1)} %get-tuple-element.470), channel_id=1, source_target_pairs={{0,16},{16,32},{32,48},{48,64},{64,80},{80,96},{96,112},{112,128},... | collective-permute-start | bytes 276488 | tf_op jit(solution)/shard_map/ppermute | solution.py:23
  409.1 8.1 %collective-permute-start.1 = (f32[5,9,4,1,128]{4,3,0,2,1:T(1,128)S(1)}, f32[5,9,4,1,128]{4,3,0,2,1:T(1,128)S(1)}, u32[]{:S(2)}, u32[]{:S(2)}) collective-permute-start(f32[5,9,4,1,128]{4,3,0,2,1:T(1,128)S(1)} %get-tuple-element.471), channel_id=1, source_target_pairs={{16,0},{32,16},{48,32},{64,48},{80,64},{96,80},{112,96},{128,112},... | collective-permute-start | bytes 276488 | tf_op jit(solution)/shard_map/ppermute | solution.py:25
  426.0 15.7 %collective-permute-start.3 = (f32[5,9,4,18,1]{3,2,4,1,0:T(4,128)S(1)}, f32[5,9,4,18,1]{3,2,4,1,0:T(4,128)S(1)}, u32[]{:S(2)}, u32[]{:S(2)}) collective-permute-start(f32[5,9,4,18,1]{3,2,4,1,0:T(4,128)S(1)} %copy.183), channel_id=1, source_target_pairs={{1,0},{2,1},{3,2},{4,3},{5,4},{6,5},{7,6},{8,7},{9,8},{10,9},{11,1... | collective-permute-start | bytes 38888 | tf_op jit(solution)/shard_map/ppermute | solution.py:25
  431.7 7.4 %collective-permute-start.2 = (f32[5,9,4,18,1]{3,2,4,1,0:T(4,128)S(1)}, f32[5,9,4,18,1]{3,2,4,1,0:T(4,128)S(1)}, u32[]{:S(2)}, u32[]{:S(2)}) collective-permute-start(f32[5,9,4,18,1]{3,2,4,1,0:T(4,128)S(1)} %copy.182), channel_id=1, source_target_pairs={{0,1},{1,2},{2,3},{3,4},{4,5},{5,6},{6,7},{7,8},{8,9},{9,10},{10,1... | collective-permute-start | bytes 38888 | tf_op jit(solution)/shard_map/ppermute | solution.py:23
  500.2 15.4 %all-to-all-start.2 = ((f32[16,1,1440]{2,1,0:T(1,128)}), f32[16,1,1440]{2,1,0:T(1,128)S(1)}, u32[]{:S(2)}, u32[]{:S(2)}) async-start(f32[16,1,1440]{2,1,0:T(1,128)} %reshape.1748), calls=%async_computation.2 | async-start | bytes 196608 | tf_op jit(solution)/shard_map/all_to_all | solution.py:173
  555.5 20.1 %all-to-all-start.3 = ((f32[16,1,5760]{2,1,0:T(1,128)}), f32[16,1,5760]{2,1,0:T(1,128)S(1)}, u32[]{:S(2)}, u32[]{:S(2)}) async-start(f32[16,1,5760]{2,1,0:T(1,128)} %reshape.1750), calls=%async_computation.3 | async-start | bytes 737280 | tf_op jit(solution)/shard_map/all_to_all | solution.py:172
  567.6 4.0 copy-start.4
  582.6 1.6 copy-start.3
  582.6 1.4 copy-start.2
  584.0 0.7 copy-start.5
Sparse Core Ops, SparseCore 0:
  277.8 118.2 reduce-scatter.3
  401.2 88.0 all-gather.1
where the time goes:
time: 616 us; the launch traced here: 609 us
  waiting for transfers between devices  178 us (29%)
  loops' own time  167 us (27%)
  other arithmetic  70.8 us (11%)
  matrix products  66.9 us (11%)
  local copies, waits for them, and re-layouts  61.4 us (10%)
  starting transfers between devices  50.4 us (8%)
  between operations  14.8 us (2%)
    another operation x1, loops' own time, legendre_matrix(): lax.scan(advance, (zero_rows, zero_rows), jnp.arange(harmonic_degree_tota...  167 us
    unnamed x3, waiting for transfers between devices  117 us
    all_gather x1, waiting for transfers between devices, shards(): portion = lax.all_gather(bent_coef, 'lat', axis=0, tiled=True)  45 us
    dot_general x1, matrix products, synthesise_lon(): return jnp.einsum('jfc,ck->jfk', gathered, order_basis, precision=highest)  24.1 us
    while x240, other arithmetic  22 us
    dot_general x1, matrix products, analyse_lon(): return jnp.einsum('jfk,kc->jfc', gathered, fourier_basis, precision=highest)  19.7 us
    all_to_all x2, starting transfers between devices, regroup(): lax.all_to_all(block_rows, 'lon', split_axis=0, concat_axis=2, tiled=True)  19.1 us
    unnamed x31, local copies, waits for them, and re-layouts  16.9 us
  transfers between devices with their start and end apart: 10, of which 5 were waited for; matrix products, arithmetic and copies ran while one was open for 14% of the time, Pallas kernels for 0%

commit v1 on v0

v1 whole, which is shorter than its diff:
```python
import functools
import math

import jax
import jax.numpy as jnp
import ml_dtypes
import numpy as np
from jax import lax
from jax.experimental import pallas as pl
from jax.experimental.pallas import tpu as pltpu
from jax.sharding import PartitionSpec as P

VARS, INST, RAD, NLAT, NLON, MODES = 5, 9, 4, 512, 2048, 256
FIELDS = VARS * INST
ROWS = 48
LATS, LONS = 32, 16
MESH = pl.DeviceIdType.MESH
f32, bf16 = jnp.float32, jnp.bfloat16
start_floor = -36.0


def split_table(table):
    high = table.astype(ml_dtypes.bfloat16)
    low = (table - high.astype(np.float64)).astype(ml_dtypes.bfloat16)
    return high, low


def circle_table():
    k = np.arange(128)
    table = np.zeros((LONS, 8, 3, 2, 128))
    for p in range(LONS):
        up = 2 * np.pi * p * k / 128
        down = -2 * np.pi * (p + 1) * k / 128
        rows = np.array(
            [
                [np.cos(up), np.sin(up)],
                [-np.sin(up), np.cos(up)],
                [np.cos(down), np.sin(down)],
                [np.sin(down), -np.cos(down)],
            ]
        )
        table[p, 0:4, 0] = rows
        table[p, 4:8, 1] = rows
        half = 2 * np.pi * (16 * p + 8) * k / 2048
        table[p, 4, 2, 0] = np.cos(up)
        table[p, 5, 2, 0] = -np.sin(up)
        table[p, 6, 2, 1] = np.cos(half)
        table[p, 7, 2, 1] = -np.sin(half)
    return table.reshape(LONS * 8, 768)


def twiddle_table():
    r = np.arange(8)[:, None]
    angle = 2 * np.pi * r * np.arange(128)[None] / 2048
    return np.concatenate([np.cos(angle), np.sin(angle)])


def time_tables():
    basis = np.zeros((9, 9))
    swapped = np.zeros((9, 9))
    s = np.arange(9)
    basis[:, 0] = 1
    for n in range(1, 5):
        c, d = np.cos(2 * np.pi * n * s / 9), np.sin(2 * np.pi * n * s / 9)
        basis[:, 2 * n - 1], basis[:, 2 * n] = c, d
        swapped[:, 2 * n - 1], swapped[:, 2 * n] = d, c
    eye = np.eye(VARS)
    both = np.zeros((45, 128))
    both[:, 0:45] = np.kron(eye, basis)
    both[:, 64:109] = np.kron(eye, swapped)
    into = np.zeros((256, 128))
    into[0:45] = both
    into[192:237] = both
    back = np.zeros((128, 128))
    for a in (0, 64):
        for b in (0, 64):
            back[a : a + 45, b : b + 45] = np.kron(eye, basis.T)
    return into, back


def ratio_rows():
    rows = np.zeros((16, 128))
    for v in range(VARS):
        rows[0, 9 * v] = 1 / 9
        for n in range(1, 5):
            rows[n, 9 * v + 2 * n - 1] = rows[n, 9 * v + 2 * n] = 2 / 9
            rows[4 + n, 64 + 9 * v + 2 * n - 1] = 2 / 9
            rows[4 + n, 64 + 9 * v + 2 * n] = -2 / 9
    return rows


def latitude_rows():
    column = np.arange(256)
    j = np.stack([16 * (column // 8) + 8 * h + column % 8 for h in (0, 1)])
    angle = (j.reshape(4, 128) + 0.5) * np.pi / NLAT
    angle = np.concatenate([angle, angle])
    return np.concatenate([np.cos(angle), np.sin(angle)])


def start_logs():
    return np.array(
        [
            0.5
            * (
                math.log((2 * m + 1) / (4 * math.pi))
                + math.lgamma(m + 0.5)
                - math.lgamma(m + 1.0)
                - 0.5 * math.log(math.pi)
            )
            for m in range(MODES)
        ]
    )


SPECTRAL = [0.5 * (-1) ** lag / math.sin(math.pi * lag / 9) for lag in range(1, 5)]


def split(value):
    high = value.astype(bf16)
    return high, (value - high.astype(f32)).astype(bf16)


def dot3(a, b):
    dot = functools.partial(jnp.dot, preferred_element_type=f32)
    return dot(a[0], b[0]) + (dot(a[0], b[1]) + dot(a[1], b[0]))


def weigh(terms):
    total = None
    for factor, value in terms:
        if abs(factor) < 1e-9:
            continue
        if abs(factor - 1) < 1e-9:
            total = value if total is None else total + value
        elif abs(factor + 1) < 1e-9:
            total = -value if total is None else total - value
        else:
            total = factor * value if total is None else total + factor * value
    return total


def sixteen(first, eighth, even, odd):
    cos = lambda n: math.cos(math.pi * n / 8)
    sin = lambda n: math.sin(math.pi * n / 8)
    plus, minus = first + eighth, first - eighth
    even_p = {d: even[d] + even[8 - d] for d in (1, 2, 3)}
    even_m = {d: even[d] - even[8 - d] for d in (1, 2, 3)}
    odd_p = {d: odd[d] + odd[8 - d] for d in (1, 2, 3)}
    odd_m = {d: odd[d] - odd[8 - d] for d in (1, 2, 3)}
    c, s = {}, {}
    for r in range(9):
        if r % 2 == 0:
            c[r] = weigh(
                [(1, plus), (cos(4 * r), even[4])] + [(cos(r * d), even_p[d]) for d in even_p]
            )
        else:
            c[r] = weigh([(1, minus)] + [(cos(r * d), even_m[d]) for d in even_m])
    for r in range(1, 8):
        if r % 2 == 0:
            s[r] = weigh([(sin(r * d), odd_m[d]) for d in odd_m])
        else:
            s[r] = weigh([(sin(4 * r), odd[4])] + [(sin(r * d), odd_p[d]) for d in odd_p])
    return c, s


def exchange(axis, me, count, send, recv, send_sem, recv_sem):
    def one(step, carry):
        peer = lax.rem(me + step, count)
        pltpu.make_async_remote_copy(
            src_ref=send.at[peer],
            dst_ref=recv.at[me],
            send_sem=send_sem,
            recv_sem=recv_sem,
            device_id={axis: peer},
            device_id_type=MESH,
        ).start()
        return carry

    lax.fori_loop(1, count, one, 0)


def drain(buffer, count, sem):
    part = buffer.at[pl.ds(0, count - 1)]
    pltpu.make_async_copy(part, part, sem).wait()


def far_field(
    x_hbm, jlat, jlon, jrad, cut, logs, real, imag,
    fwd_h, fwd_l, inv_h, inv_l, into_h, into_l, back_h, back_l, small_hbm,
    base_hbm, normal_hbm,
    shell, xv, base, s1, r1, s2, r2, s3, r3, s4, r4, s5, r5, s6, r6,
    row_send, row_recv, col_send, col_recv,
    circles, lines, raw, t_h, t_l, tt_h, tt_l, grow, drop, seed, mult,
    fwd_hv, fwd_lv, inv_hv, inv_lv, into_hv, into_lv, back_hv, back_lv, small,
    send_sem, recv_sem, halo_send, halo_recv, local,
):
    b = lax.axis_index("lat")
    p = lax.axis_index("lon")

    get_shell = pltpu.make_async_copy(x_hbm.at[:, 3], shell.at[pl.ds(0, FIELDS)], local.at[0])
    get_all = pltpu.make_async_copy(x_hbm, xv, local.at[1])
    get_shell.start()
    get_all.start()
    pairs = [
        (small_hbm, small), (fwd_h, fwd_hv), (fwd_l, fwd_lv), (inv_h, inv_hv), (inv_l, inv_lv),
        (into_h, into_hv), (into_l, into_lv), (back_h, back_hv), (back_l, back_lv),
    ]
    tables = [
        pltpu.make_async_copy(src, dst, local.at[2 + i]) for i, (src, dst) in enumerate(pairs)
    ]
    for copy in tables:
        copy.start()

    barrier = pltpu.get_barrier_semaphore()

    def greet(axis, me, count):
        def one(step, carry):
            pl.semaphore_signal(
                barrier, inc=1, device_id={axis: lax.rem(me + step, count)}, device_id_type=MESH
            )
            return carry

        lax.fori_loop(1, count, one, 0)

    greet("lon", p, LONS)
    greet("lat", b, LATS)

    shell[pl.ds(FIELDS, ROWS - FIELDS)] = jnp.zeros((ROWS - FIELDS, 16, 128), f32)
    get_shell.wait()
    shell_rows = shell.reshape(ROWS * 16, 128)
    for j in range(16):
        s1[j] = shell_rows[pl.ds(j, ROWS, stride=16), :]
    r1[p] = s1[p]
    pl.semaphore_wait(barrier, LONS + LATS - 2)
    exchange("lon", p, LONS, s1, r1, send_sem.at[0], recv_sem.at[0])

    get_all.wait()
    lane = lax.broadcasted_iota(jnp.int32, (16, 128), 1)
    row = lax.broadcasted_iota(jnp.int32, (16, 128), 0)
    x_rows = xv.reshape(FIELDS * RAD * 16, 128)
    row_send[0] = x_rows[pl.ds(0, 180, stride=16), :]
    row_send[1] = x_rows[pl.ds(15, 180, stride=16), :]

    def halo(axis, peer, index, send, recv):
        return pltpu.make_async_remote_copy(
            src_ref=send,
            dst_ref=recv,
            send_sem=halo_send.at[index],
            recv_sem=halo_recv.at[index],
            device_id={axis: peer},
            device_id_type=MESH,
        )

    halos = [
        halo("lat", lax.rem(b + LATS - 1, LATS), 0, row_send.at[0], row_recv.at[0]),
        halo("lat", lax.rem(b + 1, LATS), 1, row_send.at[1], row_recv.at[1]),
        halo("lon", lax.rem(p + LONS - 1, LONS), 2, col_send.at[0], col_recv.at[0]),
        halo("lon", lax.rem(p + 1, LONS), 3, col_send.at[1], col_recv.at[1]),
    ]
    halos[0].start()
    halos[1].start()

    def pack(f, packed):
        packed = list(packed)
        for r in range(RAD):
            x = xv[f, r]
            at = f + 64 * (r % 2)
            here = lane == at
            for side in (0, 1):
                i = 2 * side + r // 2
                packed[i] = jnp.where(here, pltpu.roll(x, lax.rem(at + side, 128), 1), packed[i])
        return tuple(packed)

    packed = lax.fori_loop(0, FIELDS, pack, (jnp.zeros((16, 128), f32),) * 4)
    for i in range(4):
        col_send[i // 2, i % 2] = packed[i]
    halos[2].start()
    halos[3].start()

    rho, g = b // 4, b % 4
    r = jnp.where(rho < 4, 2 * g + 1, 2 * g + 2)
    m = jnp.where(rho % 4 < 2, 16 * p + r, 16 * p + 16 - r)
    m = jnp.where((g == 3) & (rho >= 4), 16 * p + 8 * ((rho - 4) // 2), m)
    tables[0].wait()
    degree = lax.broadcasted_iota(jnp.int32, (MODES, 128), 0)
    deg = degree.astype(f32)
    order = m.astype(f32)
    order2 = order * order

    def factor(d):
        return jnp.sqrt(
            jnp.maximum(4.0 * d * d - 1.0, 1.0) / jnp.maximum(d * d - order2, 1.0)
        )

    factor_now, factor_prev = factor(deg), factor(deg - 1.0)
    grow[...] = jnp.where(degree > m, factor_now, 0.0)
    drop[...] = jnp.where(degree > m + 1, factor_now / factor_prev, 0.0)
    seed[...] = jnp.where(degree == m, 1.0, 0.0)
    cosine, sine_all = small[0:8], small[8:16]
    log_diagonal = logs[m] + order * jnp.log(sine_all)
    diagonal = jnp.where(
        log_diagonal >= start_floor, jnp.exp(jnp.maximum(log_diagonal, start_floor)), 0.0
    )

    def advance(i, state):
        latest, before = state
        first = pl.multiple_of(i * 8, 8)
        a8, q8, d8 = grow[pl.ds(first, 8)], drop[pl.ds(first, 8)], seed[pl.ds(first, 8)]
        for n in range(8):
            step = a8[n : n + 1] * cosine
            rest = d8[n : n + 1] * diagonal - q8[n : n + 1] * before
            latest, before = step * latest + rest, latest
            raw[pl.ds(pl.multiple_of((first + n) * 8, 8), 8)] = latest
        return latest, before

    zero = jnp.zeros((8, 128), f32)
    lax.fori_loop(0, MODES // 8, advance, (zero, zero))
    for s in range(4):
        h, half = s // 2, s % 2
        block = raw[pl.ds(s, MODES, stride=8), :]
        high, low = split(block)
        t_h[pl.ds(h * 256, 256), pl.ds(half * 128, 128)] = high
        t_l[pl.ds(h * 256, 256), pl.ds(half * 128, 128)] = low
        high, low = split(block.T)
        tt_h[pl.ds(half * 128, 128), pl.ds(h * 256, 256)] = high
        tt_l[pl.ds(half * 128, 128), pl.ds(h * 256, 256)] = low

    factors = jnp.zeros((MODES, 128), f32)
    for n in range(5):
        kept = jnp.where(degree <= cut[n], real[:, n : n + 1], 0.0)
        factors = factors + kept * small[32 + n : 33 + n]
        if n:
            kept = jnp.where(degree <= cut[n], imag[:, n - 1 : n], 0.0)
            factors = factors + kept * small[36 + n : 37 + n]
    mult[...] = factors * jnp.where(m == 0, 1.0, 2.0)

    j_own = 16 * b + p
    term = (
        lax.broadcasted_iota(jnp.int32, (8, 128), 0) * 128
        + lax.broadcasted_iota(jnp.int32, (8, 128), 1)
        + 1
    )
    angle = ((term * (2 * j_own + 1)) & (2 * NLAT - 1)).astype(f32) * (math.pi / NLAT)
    termf = term.astype(f32)
    part = jnp.where(term <= NLAT // 2, jnp.cos(angle) / (4.0 * termf * termf - 1.0), 0.0)
    series = jnp.sum(jnp.sum(part, axis=1, keepdims=True), axis=0, keepdims=True)
    weight = (2.0 / NLAT) * (1.0 - 2.0 * series) * (2.0 * math.pi / NLON)

    for i in (2, 3, 0, 1):
        halos[i].wait_recv()
    band = (16 * b + row).astype(f32)
    sine = jnp.sin((band + 0.5) * (math.pi / NLAT))
    half_sine = 0.5 * sine
    south_keep = jnp.where(b == LATS - 1, 0.0, 1.0)
    north_keep = jnp.where(b == 0, 0.0, 1.0)
    jl = [[jlat[v, w] for w in range(VARS)] for v in range(VARS)]
    jo = [[jlon[v, w] for w in range(VARS)] for v in range(VARS)]
    jr = [[jrad[v, w] for w in range(VARS)] for v in range(VARS)]

    def one_instance(t, carry):
        for r in range(RAD):
            lat_d, rad_d, lon_d, rest = [], [], [], []
            for w in range(VARS):
                f = w * INST + t
                x = xv[f, r]
                index = f * RAD + r
                at = f + 64 * (r % 2)
                south_row = row_recv[0, pl.ds(index, 1)] * south_keep
                north_row = row_recv[1, pl.ds(index, 1)] * north_keep
                south = jnp.where(row == 15, south_row, pltpu.roll(x, 15, 0))
                north = jnp.where(row == 0, north_row, pltpu.roll(x, 1, 0))
                east_col = pltpu.roll(col_recv[0, r // 2], 127 - at, 1)
                west_col = pltpu.roll(col_recv[1, r // 2], lax.rem(128 - at, 128), 1)
                east = jnp.where(lane == 127, east_col, pltpu.roll(x, 127, 1))
                west = jnp.where(lane == 0, west_col, pltpu.roll(x, 1, 1))
                above = xv[f, r + 1] if r < RAD - 1 else x
                below = xv[f, r - 1] if r > 0 else jnp.zeros_like(x)
                lat_d.append(half_sine * (south - north))
                rad_d.append(half_sine * (above - below))
                lon_d.append(0.5 * (east - west))
                spread = half_sine * (south + north + above + below - 4.0 * x)
                timing = -spread - 0.5 * (east + west - 2.0 * x)
                for lag in range(1, 5):
                    back = xv[w * INST + lax.rem(t + 9 - lag, 9), r]
                    ahead = xv[w * INST + lax.rem(t + lag, 9), r]
                    timing = timing + SPECTRAL[lag - 1] * (back - ahead)
                rest.append(timing)
            for v in range(VARS):
                total = rest[v]
                for w in range(VARS):
                    total = total + (
                        jl[v][w] * lat_d[w] + jr[v][w] * rad_d[w] + jo[v][w] * lon_d[w]
                    )
                base[v * INST + t, r] = total
        return carry

    lax.fori_loop(0, INST, one_instance, 0)
    put_base = pltpu.make_async_copy(base, base_hbm, local.at[0])
    put_base.start()

    for g4 in range(4):
        circles[pl.ds(64 * g4 + ROWS, 64 - ROWS)] = jnp.zeros((64 - ROWS, 768), f32)
    circles[pl.ds(0, 192), pl.ds(512, 256)] = jnp.zeros((192, 256), f32)
    circles[pl.ds(192, 64), pl.ds(256, 256)] = jnp.zeros((64, 256), f32)
    tw = lambda r: (small[16 + r : 17 + r], small[24 + r : 25 + r])
    for copy in tables[1:]:
        copy.wait()
    drain(r1, LONS, recv_sem.at[0])

    def analyse(i, carry):
        first = pl.multiple_of(i * 8, 8)
        x = [r1[d, pl.ds(first, 8)] for d in range(16)]
        even = {d: x[d] + x[16 - d] for d in range(1, 8)}
        odd = {d: x[d] - x[16 - d] for d in range(1, 8)}
        c, s = sixteen(x[0], x[8], even, odd)
        for r in range(1, 8):
            co, si = tw(r)
            at = pl.ds(64 * ((r - 1) // 2) + first, 8)
            column = 256 * ((r - 1) % 2)
            circles[at, pl.ds(column, 128)] = c[r] * co - s[r] * si
            circles[at, pl.ds(column + 128, 128)] = -s[r] * co - c[r] * si
        at = pl.ds(192 + first, 8)
        circles[at, pl.ds(512, 128)] = c[0]
        circles[at, pl.ds(640, 128)] = c[8]
        return carry

    lax.fori_loop(0, ROWS // 8, analyse, 0)
    found = dot3(split(circles[...]), (fwd_hv[...], fwd_lv[...])) * weight
    for half in (0, 1):
        s2[:, pl.ds(8 * half, 8), :] = found[128 * half : 128 * half + 128].T.reshape(16, 8, 128)
    r2[p] = s2[p]
    exchange("lon", p, LONS, s2, r2, send_sem.at[1], recv_sem.at[1])

    low_half = lax.broadcasted_iota(jnp.int32, (8, 128), 1) < 64
    drain(r2, LONS, recv_sem.at[1])
    r2_rows = r2.reshape(256, 128)
    for rho8 in range(8):
        for half in (0, 1):
            north8 = r2_rows[pl.ds(8 * half + rho8, 8, stride=16), :]
            south8 = r2_rows[pl.ds(128 + 8 * half + rho8, 8, stride=16), :]
            s3[4 * rho8 + 2 * half] = jnp.where(low_half, north8, pltpu.roll(south8, 64, 1))
            s3[4 * rho8 + 2 * half + 1] = jnp.where(low_half, pltpu.roll(north8, 64, 1), south8)
    r3[b] = s3[b]
    exchange("lat", b, LATS, s3, r3, send_sem.at[2], recv_sem.at[2])
    drain(r3, LATS, recv_sem.at[2])

    degrees = dot3((t_h[...], t_l[...]), split(r3[...].reshape(256, 128)))
    degrees = jnp.concatenate([degrees[0:256], degrees[256:512]], axis=1)
    modes = dot3(split(degrees), (into_hv[...], into_lv[...])) * mult[...]
    bent = dot3(split(modes), (back_hv[...], back_lv[...]))
    left = lax.broadcasted_iota(jnp.int32, (MODES, 128), 1) < 64
    bent = jnp.concatenate([jnp.where(left, bent, 0.0), jnp.where(left, 0.0, bent)], axis=0)
    s4[...] = dot3((tt_h[...], tt_l[...]), split(bent)).reshape(32, 8, 128)
    r4[b] = s4[b]
    exchange("lat", b, LATS, s4, r4, send_sem.at[3], recv_sem.at[3])
    drain(r4, LATS, recv_sem.at[3])

    s5_rows = s5.reshape(256, 128)
    for rho8 in range(8):
        for half in (0, 1):
            one, two = r4[4 * rho8 + 2 * half], r4[4 * rho8 + 2 * half + 1]
            s5_rows[pl.ds(8 * half + rho8, 8, stride=16), :] = jnp.where(
                low_half, one, pltpu.roll(two, 64, 1)
            )
            s5_rows[pl.ds(128 + 8 * half + rho8, 8, stride=16), :] = jnp.where(
                low_half, pltpu.roll(one, 64, 1), two
            )
    r5[p] = s5[p]
    exchange("lon", p, LONS, s5, r5, send_sem.at[4], recv_sem.at[4])
    drain(r5, LONS, recv_sem.at[4])

    found = jnp.concatenate(
        [r5[:, pl.ds(8 * half, 8), :].reshape(128, 128).T for half in (0, 1)], axis=0
    )
    lines[...] = dot3(split(found), (inv_hv[...], inv_lv[...]))

    def synthesise(i, carry):
        first = pl.multiple_of(i * 8, 8)
        even, odd = {}, {}
        for r in range(1, 8):
            co, si = tw(r)
            at = pl.ds(64 * ((r - 1) // 2) + first, 8)
            column = 256 * ((r - 1) % 2)
            re, im = lines[at, pl.ds(column, 128)], lines[at, pl.ds(column + 128, 128)]
            even[r] = re * co - im * si
            odd[r] = re * si + im * co
        at = pl.ds(192 + first, 8)
        c, s = sixteen(lines[at, pl.ds(512, 128)], lines[at, pl.ds(640, 128)], even, odd)
        s6[0, pl.ds(first, 8)] = c[0]
        s6[8, pl.ds(first, 8)] = c[8]
        for d in range(1, 8):
            s6[d, pl.ds(first, 8)] = c[d] - s[d]
            s6[16 - d, pl.ds(first, 8)] = c[d] + s[d]
        return carry

    lax.fori_loop(0, ROWS // 8, synthesise, 0)
    r6[p] = s6[p]
    exchange("lon", p, LONS, s6, r6, send_sem.at[5], recv_sem.at[5])
    drain(r6, LONS, recv_sem.at[5])
    put_normal = pltpu.make_async_copy(r6, normal_hbm, local.at[1])
    put_normal.start()
    for i, (buffer, count) in enumerate(
        [(s1, LONS), (s2, LONS), (s3, LATS), (s4, LATS), (s5, LONS), (s6, LONS)]
    ):
        drain(buffer, count, send_sem.at[i])
    for copy in halos:
        copy.wait_send()
    put_base.wait()
    put_normal.wait()


def finish(base_hbm, circles, jrad, out_hbm, normal, layer, sem):
    b = lax.axis_index("lat")
    inner = pltpu.make_async_copy(
        base_hbm.at[:, pl.ds(0, 3)], out_hbm.at[:, pl.ds(0, 3)], sem.at[0]
    )
    inner.start()
    get = pltpu.make_async_copy(base_hbm.at[:, 3], layer, sem.at[1])
    get.start()
    row = lax.broadcasted_iota(jnp.int32, (16, 128), 0)
    half_sine = 0.5 * jnp.sin(((16 * b + row).astype(f32) + 0.5) * (math.pi / NLAT))
    jr = [[jrad[v, w] for w in range(VARS)] for v in range(VARS)]
    rows = circles.reshape(16 * ROWS, 128)
    get.wait()

    def one_instance(t, carry):
        n = []
        for w in range(VARS):
            value = rows[pl.ds(w * INST + t, 16, stride=ROWS), :]
            normal[w * INST + t] = value
            n.append(value)
        for v in range(VARS):
            total = -n[v]
            for w in range(VARS):
                total = total + jr[v][w] * n[w]
            layer[v * INST + t] = layer[v * INST + t] + half_sine * total
        return carry

    lax.fori_loop(0, INST, one_instance, 0)
    put = pltpu.make_async_copy(layer, out_hbm.at[:, 3], sem.at[1])
    put.start()
    put.wait()
    inner.wait()


def shards(flow_state, jacobian_lat, jacobian_lon, jacobian_rad, ratio_real, ratio_imag, cut):
    x = flow_state.reshape(FIELDS, RAD, 16, 128)
    table = circle_table()
    into, back = time_tables()
    small = np.zeros((48, 128), np.float32)
    small[0:16] = latitude_rows()
    small[16:32] = twiddle_table()
    small[32:48] = ratio_rows()
    logs = start_logs().astype(np.float32)
    constants = [
        jnp.asarray(part)
        for full in (table.T, table, into, back)
        for part in split_table(np.ascontiguousarray(full))
    ] + [jnp.asarray(small)]
    smem = pl.BlockSpec(memory_space=pltpu.SMEM)
    vmem = pl.BlockSpec(memory_space=pltpu.VMEM)
    hbm = pl.BlockSpec(memory_space=pl.ANY)
    v = lambda *shape: pltpu.VMEM(shape, f32)
    w = lambda *shape: pltpu.VMEM(shape, bf16)
    base, circles = pl.pallas_call(
        far_field,
        out_shape=[
            jax.ShapeDtypeStruct((FIELDS, RAD, 16, 128), f32),
            jax.ShapeDtypeStruct((16, ROWS, 128), f32),
        ],
        in_specs=[hbm] + [smem] * 5 + [vmem] * 2 + [hbm] * len(constants),
        out_specs=[hbm, hbm],
        scratch_shapes=[
            v(ROWS, 16, 128), v(FIELDS, RAD, 16, 128), v(FIELDS, RAD, 16, 128),
            v(16, ROWS, 128), v(16, ROWS, 128),
            v(16, 16, 128), v(16, 16, 128),
            v(32, 8, 128), v(32, 8, 128),
            v(32, 8, 128), v(32, 8, 128),
            v(16, 16, 128), v(16, 16, 128),
            v(16, ROWS, 128), v(16, ROWS, 128),
            v(2, 180, 128), v(2, 180, 128), v(2, 2, 16, 128), v(2, 2, 16, 128),
            v(256, 768), v(256, 768), v(MODES * 8, 128),
            w(512, 256), w(512, 256), w(256, 512), w(256, 512),
            v(MODES, 128), v(MODES, 128), v(MODES, 128), v(MODES, 128),
            w(768, 128), w(768, 128), w(128, 768), w(128, 768),
            w(256, 128), w(256, 128), w(128, 128), w(128, 128), v(48, 128),
            pltpu.SemaphoreType.DMA((6,)), pltpu.SemaphoreType.DMA((6,)),
            pltpu.SemaphoreType.DMA((4,)), pltpu.SemaphoreType.DMA((4,)),
            pltpu.SemaphoreType.DMA((11,)),
        ],
        compiler_params=pltpu.CompilerParams(
            collective_id=0, has_side_effects=True, vmem_limit_bytes=40 * 1024 * 1024
        ),
        name="far_field",
    )(x, jacobian_lat, jacobian_lon, jacobian_rad, cut, jnp.asarray(logs), ratio_real, ratio_imag,
      *constants)
    residual, normal = pl.pallas_call(
        finish,
        out_shape=[
            jax.ShapeDtypeStruct((FIELDS, RAD, 16, 128), f32),
            jax.ShapeDtypeStruct((FIELDS, 16, 128), f32),
        ],
        in_specs=[hbm, vmem, smem],
        out_specs=[hbm, vmem],
        scratch_shapes=[v(FIELDS, 16, 128), pltpu.SemaphoreType.DMA((2,))],
        compiler_params=pltpu.CompilerParams(vmem_limit_bytes=16 * 1024 * 1024),
        name="finish",
    )(base, circles, jacobian_rad)
    return (
        residual.reshape(VARS, INST, RAD, 16, 128),
        normal.reshape(VARS, INST, 16, 128),
    )


def solution(mesh):
    placed = (P(None, None, None, "lat", "lon"), P(), P(), P(), P(), P(), P())
    return jax.shard_map(
        shards,
        mesh=mesh,
        in_specs=placed,
        out_specs=(P(None, None, None, "lat", "lon"), P(None, None, "lat", "lon")),
        check_vma=False,
    )
```

time: 616 us -> 92.7 us (0.15)
  the two profiles are of different devices: /device:TPU:1 before, /device:TPU:2 now
where the time goes in v1:
time: 92.7 us; the launch traced here: 91.9 us
  Pallas kernels  77.2 us (83%)
  local copies, waits for them, and re-layouts  14 us (15%)
    pallas_call x1, Pallas kernels, shards(): pl.pallas_call(far_field, out_shape=[jax.ShapeDtypeStruct((FIELDS, RAD, 1...  74.7 us
    unnamed x32, local copies, waits for them, and re-layouts  14 us
    pallas_call x1, Pallas kernels, shards(): pl.pallas_call(finish, out_shape=[jax.ShapeDtypeStruct((FIELDS, RAD, 16,...  2.46 us

profile of v1, /device:TPU:2, one launch (start us, length us, event | category | flops | bytes accessed | tf_op | source)
XLA Modules:
  0.0 91.9 jit_solution(13540229033773906259)
XLA Ops:
  0.6 0.8 copy.19.real
  1.5 0.8 copy.20.imag
  2.3 0.0 copy-start
  2.3 1.4 %copy-done = f32[5,9,4,16,128]{4,3,2,1,0:T(8,128)S(1)} copy-done((f32[5,9,4,16,128]{4,3,2,1,0:T(8,128)S(1)}, f32[5,9,4,16,128]{4,3,2,1,0:T(8,128)}, u32[]{:S(2)}) %copy-start) | copy-done | bytes 1474584
  3.7 0.0 copy-start.1
  3.7 0.9 %copy-done.1 = bf16[128,768]{1,0:T(8,128)(2,1)S(1)} copy-done((bf16[128,768]{1,0:T(8,128)(2,1)S(1)}, bf16[128,768]{1,0:T(8,128)(2,1)}, u32[]{:S(2)}) %copy-start.1) | copy-done | bytes 196632
  4.6 0.0 copy-start.2
  4.6 0.9 %copy-done.2 = bf16[128,768]{1,0:T(8,128)(2,1)S(1)} copy-done((bf16[128,768]{1,0:T(8,128)(2,1)S(1)}, bf16[128,768]{1,0:T(8,128)(2,1)}, u32[]{:S(2)}) %copy-start.2) | copy-done | bytes 196632
  5.5 0.0 copy-start.3
  5.5 0.9 %copy-done.3 = bf16[768,128]{1,0:T(8,128)(2,1)S(1)} copy-done((bf16[768,128]{1,0:T(8,128)(2,1)S(1)}, bf16[768,128]{1,0:T(8,128)(2,1)}, u32[]{:S(2)}) %copy-start.3) | copy-done | bytes 196632
  6.4 0.0 copy-start.4
  6.5 0.9 %copy-done.4 = bf16[768,128]{1,0:T(8,128)(2,1)S(1)} copy-done((bf16[768,128]{1,0:T(8,128)(2,1)S(1)}, bf16[768,128]{1,0:T(8,128)(2,1)}, u32[]{:S(2)}) %copy-start.4) | copy-done | bytes 196632
  7.4 0.0 copy-start.5
  7.4 0.8 copy-done.5
  8.2 0.0 copy-start.6
  8.2 0.8 copy-done.6
  9.1 0.0 copy-start.7
  9.1 0.8 copy-done.7
  9.8 0.0 copy-start.8
  9.8 0.8 copy-done.8
  10.6 0.0 copy-start.9
  10.6 0.7 copy-done.9
  11.3 0.0 copy-start.10
  11.3 0.7 copy-done.10
  12.0 0.0 copy-start.11
  12.0 0.7 copy-done.11
  12.7 0.0 copy-start.12
  12.7 0.7 copy-done.12
  13.4 0.0 copy-start.13
  13.4 0.7 copy-done.13
  14.1 0.0 copy-start.14
  14.1 0.7 copy-done.14
  14.7 74.7 %far_field.1 = (f32[45,4,16,128]{3,2,1,0:T(8,128)S(1)}, f32[16,48,128]{2,1,0:T(8,128)S(1)}) custom-call(f32[45,4,16,128]{3,2,1,0:T(8,128)S(1)} %bitcast.3, f32[5,5]{1,0:T(8,128)S(1)} %copy-done.11, f32[5,5]{1,0:T(8,128)S(1)} %copy-done.12, f32[5,5]{1,0:T(8,128)S(1)} %copy-done.10, s32[5]{0:T(128)S(1)} %copy-done.14, f32[256]{0:T(256)S(1)} %copy-done.13, ...), custom_call_target="tpu_custom_call" | custom-call | tf_op jit(solution)/shard_map/far_field/pallas_call | solution.py:565
  89.5 2.5 %finish.1 = (f32[45,4,16,128]{3,2,1,0:T(8,128)}, f32[45,16,128]{2,1,0:T(8,128)}) custom-call(f32[45,4,16,128]{3,2,1,0:T(8,128)S(1)} %get-tuple-element.6.base_hbm, f32[16,48,128]{2,1,0:T(8,128)S(1)} %get-tuple-element.7.circles, f32[5,5]{1,0:T(8,128)S(1)} %copy-done.10), custom_call_target="tpu_custom_call" | custom-call | tf_op jit(solution)/shard_map/finish/pallas_call | solution.py:597
Async XLA Ops:
  2.3 1.4 %copy-start = (f32[5,9,4,16,128]{4,3,2,1,0:T(8,128)S(1)}, f32[5,9,4,16,128]{4,3,2,1,0:T(8,128)}, u32[]{:S(2)}) copy-start(f32[5,9,4,16,128]{4,3,2,1,0:T(8,128)} %param.17) | copy-start | bytes 4423684
  3.7 0.9 %copy-start.1 = (bf16[128,768]{1,0:T(8,128)(2,1)S(1)}, bf16[128,768]{1,0:T(8,128)(2,1)}, u32[]{:S(2)}) copy-start(bf16[128,768]{1,0:T(8,128)(2,1)} %constant.23.clone.inv_l) | copy-start | bytes 589828
  4.6 0.9 %copy-start.2 = (bf16[128,768]{1,0:T(8,128)(2,1)S(1)}, bf16[128,768]{1,0:T(8,128)(2,1)}, u32[]{:S(2)}) copy-start(bf16[128,768]{1,0:T(8,128)(2,1)} %constant.22.clone.inv_h) | copy-start | bytes 589828
  5.5 0.9 %copy-start.3 = (bf16[768,128]{1,0:T(8,128)(2,1)S(1)}, bf16[768,128]{1,0:T(8,128)(2,1)}, u32[]{:S(2)}) copy-start(bf16[768,128]{1,0:T(8,128)(2,1)} %constant.21.clone.fwd_l) | copy-start | bytes 589828
  6.4 0.9 %copy-start.4 = (bf16[768,128]{1,0:T(8,128)(2,1)S(1)}, bf16[768,128]{1,0:T(8,128)(2,1)}, u32[]{:S(2)}) copy-start(bf16[768,128]{1,0:T(8,128)(2,1)} %constant.20.clone.fwd_h) | copy-start | bytes 589828
  7.4 0.8 copy-start.5
  8.2 0.8 copy-start.6
  9.1 0.8 copy-start.7
  9.8 0.8 copy-start.8
  10.6 0.7 copy-start.9
  11.3 0.7 copy-start.10
  12.0 0.7 copy-start.11
  12.7 0.7 copy-start.12
  13.4 0.7 copy-start.13
  14.1 0.7 copy-start.14

commit v2 on v1

v2 whole, which is shorter than its diff:
```python
import functools
import math

import jax
import jax.numpy as jnp
import ml_dtypes
import numpy as np
from jax import lax
from jax.experimental import pallas as pl
from jax.experimental.pallas import tpu as pltpu
from jax.sharding import PartitionSpec as P

VARS, INST, RAD, NLAT, NLON, MODES = 5, 9, 4, 512, 2048, 256
FIELDS = VARS * INST
ROWS = 48
LATS, LONS = 32, 16
MESH = pl.DeviceIdType.MESH
f32, bf16 = jnp.float32, jnp.bfloat16
start_floor = -36.0


def split_table(table):
    high = table.astype(ml_dtypes.bfloat16)
    low = (table - high.astype(np.float64)).astype(ml_dtypes.bfloat16)
    return high, low


def circle_table():
    k = np.arange(128)
    table = np.zeros((LONS, 8, 3, 2, 128))
    for p in range(LONS):
        up = 2 * np.pi * p * k / 128
        down = -2 * np.pi * (p + 1) * k / 128
        rows = np.array(
            [
                [np.cos(up), np.sin(up)],
                [-np.sin(up), np.cos(up)],
                [np.cos(down), np.sin(down)],
                [np.sin(down), -np.cos(down)],
            ]
        )
        table[p, 0:4, 0] = rows
        table[p, 4:8, 1] = rows
        half = 2 * np.pi * (16 * p + 8) * k / 2048
        table[p, 4, 2, 0] = np.cos(up)
        table[p, 5, 2, 0] = -np.sin(up)
        table[p, 6, 2, 1] = np.cos(half)
        table[p, 7, 2, 1] = -np.sin(half)
    return table.reshape(LONS * 8, 768)


def twiddle_table():
    r = np.arange(8)[:, None]
    angle = 2 * np.pi * r * np.arange(128)[None] / 2048
    return np.concatenate([np.cos(angle), np.sin(angle)])


def slot_table():
    pairs = [[(v, n, 0), (v, n, 1)] for v in range(VARS) for n in range(1, 5)]
    pairs += [[(0, 0, 0), (1, 0, 0)], [(2, 0, 0), (3, 0, 0)], [(4, 0, 0), None], [None, None]]
    return [sum(pairs[3 * z : 3 * z + 3], []) for z in range(8)]


SLOTS = slot_table()
PLACE = {item: (z, i) for z in range(8) for i, item in enumerate(SLOTS[z]) if item}


def ratio_rows():
    rows = np.zeros((8, 16, 2, 8, 8))
    for z in range(8):
        for i, item in enumerate(SLOTS[z]):
            if item is None:
                continue
            _, n, part = item
            rows[z, n, :, i] = 2 / 9 if n else 1 / 9
            if n:
                rows[z, 7 + n, :, i] = -2 / 9 if part else 2 / 9
    return rows.reshape(8, 16, 128)


def fold_time(first, even, odd):
    c, s = {}, {}
    for n in range(1, 5):
        angles = {k: 2 * math.pi * n * k / 9 for k in range(1, 5)}
        c[n] = weigh([(1, first)] + [(math.cos(angles[k]), even[k]) for k in angles])
        s[n] = weigh([(math.sin(angles[k]), odd[k]) for k in angles])
    return c, s


def latitude_rows():
    column = np.arange(256)
    j = np.stack([16 * (column // 8) + 8 * h + column % 8 for h in (0, 1)])
    angle = (j.reshape(4, 128) + 0.5) * np.pi / NLAT
    angle = np.concatenate([angle, angle])
    return np.concatenate([np.cos(angle), np.sin(angle)])


def start_logs():
    return np.array(
        [
            0.5
            * (
                math.log((2 * m + 1) / (4 * math.pi))
                + math.lgamma(m + 0.5)
                - math.lgamma(m + 1.0)
                - 0.5 * math.log(math.pi)
            )
            for m in range(MODES)
        ]
    )


SPECTRAL = [0.5 * (-1) ** lag / math.sin(math.pi * lag / 9) for lag in range(1, 5)]


def split(value):
    high = value.astype(bf16)
    return high, (value - high.astype(f32)).astype(bf16)


def dot(a, b):
    return jnp.dot(a, b, preferred_element_type=f32)


def dot_wide(a, wide):
    total = dot(a[0], wide)
    return total[:, 0:128] + (total[:, 128:256] + dot(a[1], wide[:, 0:128]))


def weigh(terms):
    total = None
    for factor, value in terms:
        if abs(factor) < 1e-9:
            continue
        if abs(factor - 1) < 1e-9:
            total = value if total is None else total + value
        elif abs(factor + 1) < 1e-9:
            total = -value if total is None else total - value
        else:
            total = factor * value if total is None else total + factor * value
    return total


def sixteen(first, eighth, even, odd):
    cos = lambda n: math.cos(math.pi * n / 8)
    sin = lambda n: math.sin(math.pi * n / 8)
    plus, minus = first + eighth, first - eighth
    even_p = {d: even[d] + even[8 - d] for d in (1, 2, 3)}
    even_m = {d: even[d] - even[8 - d] for d in (1, 2, 3)}
    odd_p = {d: odd[d] + odd[8 - d] for d in (1, 2, 3)}
    odd_m = {d: odd[d] - odd[8 - d] for d in (1, 2, 3)}
    c, s = {}, {}
    for r in range(9):
        if r % 2 == 0:
            c[r] = weigh(
                [(1, plus), (cos(4 * r), even[4])] + [(cos(r * d), even_p[d]) for d in even_p]
            )
        else:
            c[r] = weigh([(1, minus)] + [(cos(r * d), even_m[d]) for d in even_m])
    for r in range(1, 8):
        if r % 2 == 0:
            s[r] = weigh([(sin(r * d), odd_m[d]) for d in odd_m])
        else:
            s[r] = weigh([(sin(4 * r), odd[4])] + [(sin(r * d), odd_p[d]) for d in odd_p])
    return c, s


def exchange(axis, me, count, send, recv, send_sem, recv_sem):
    def one(step, carry):
        peer = lax.rem(me + step, count)
        pltpu.make_async_remote_copy(
            src_ref=send.at[peer],
            dst_ref=recv.at[me],
            send_sem=send_sem,
            recv_sem=recv_sem,
            device_id={axis: peer},
            device_id_type=MESH,
        ).start()
        return carry

    lax.fori_loop(1, count, one, 0)


def drain(buffer, count, sem):
    part = buffer.at[pl.ds(0, count - 1)]
    pltpu.make_async_copy(part, part, sem).wait()


def far_field(
    x_hbm, jlat_hbm, jlon_hbm, jrad_hbm, cut_hbm, real_hbm, imag_hbm, fwd_hbm, inv_hbm, small_hbm,
    select_hbm, base_hbm, normal_hbm,
    shell, xv, base, s1, r1, s2, r2, s3, r3, s4, r4, s5, r5, s6,
    row_send, row_recv, col_send, col_recv,
    circles, lines, raw, t_h, t_l, tt_h, tt_l, grow, drop, seed, mult,
    fwd, inv, small, select, jlat, jlon, jrad, cut, real, imag,
    send_sem, recv_sem, halo_send, halo_recv, local,
):
    b = lax.axis_index("lat")
    p = lax.axis_index("lon")
    z, x = p // 2, p % 2
    partner = p + 1 - 2 * x

    barrier = pltpu.get_barrier_semaphore()

    def greet(axis, me, count):
        def one(step, carry):
            pl.semaphore_signal(
                barrier, inc=1, device_id={axis: lax.rem(me + step, count)}, device_id_type=MESH
            )
            return carry

        lax.fori_loop(1, count, one, 0)

    greet("lon", p, LONS)
    greet("lat", b, LATS)

    get_shell = pltpu.make_async_copy(x_hbm.at[:, 3], shell, local.at[0])
    get_all = pltpu.make_async_copy(x_hbm, xv, local.at[1])
    get_shell.start()
    get_all.start()
    pairs = [
        (small_hbm, small), (real_hbm, real), (imag_hbm, imag), (cut_hbm, cut),
        (jlat_hbm, jlat), (jlon_hbm, jlon), (jrad_hbm, jrad),
        (select_hbm, select), (fwd_hbm, fwd), (inv_hbm, inv),
    ]
    tables = [
        pltpu.make_async_copy(src, dst, local.at[2 + i]) for i, (src, dst) in enumerate(pairs)
    ]
    for copy in tables:
        copy.start()

    get_shell.wait()
    for z8 in range(8):
        for i, item in enumerate(SLOTS[z8]):
            if item is None:
                for h in (0, 1):
                    s1[2 * z8 + h, pl.ds(8 * i, 8)] = jnp.zeros((8, 128), f32)
    for v in range(VARS):
        for h in (0, 1):
            q = [shell[v * INST + t, pl.ds(8 * h, 8)] for t in range(INST)]
            even = {k: q[k] + q[9 - k] for k in range(1, 5)}
            odd = {k: q[k] - q[9 - k] for k in range(1, 5)}
            c, s = fold_time(q[0], even, odd)
            parts = {(v, 0, 0): q[0] + sum(even.values())}
            for n in range(1, 5):
                parts[v, n, 0], parts[v, n, 1] = c[n], s[n]
            for item, value in parts.items():
                z8, i = PLACE[item]
                s1[2 * z8 + h, pl.ds(8 * i, 8)] = value
    r1[p] = s1[p]
    pl.semaphore_wait(barrier, LONS + LATS - 2)
    exchange("lon", p, LONS, s1, r1, send_sem.at[0], recv_sem.at[0])

    get_all.wait()
    lane = lax.broadcasted_iota(jnp.int32, (16, 128), 1)
    row = lax.broadcasted_iota(jnp.int32, (16, 128), 0)
    x_rows = xv.reshape(FIELDS * RAD * 16, 128)
    row_send[0] = x_rows[pl.ds(0, 180, stride=16), :]
    row_send[1] = x_rows[pl.ds(15, 180, stride=16), :]

    def halo(axis, peer, index, send, recv):
        return pltpu.make_async_remote_copy(
            src_ref=send,
            dst_ref=recv,
            send_sem=halo_send.at[index],
            recv_sem=halo_recv.at[index],
            device_id={axis: peer},
            device_id_type=MESH,
        )

    halos = [
        halo("lat", lax.rem(b + LATS - 1, LATS), 0, row_send.at[0], row_recv.at[0]),
        halo("lat", lax.rem(b + 1, LATS), 1, row_send.at[1], row_recv.at[1]),
        halo("lon", lax.rem(p + LONS - 1, LONS), 2, col_send.at[0], col_recv.at[0]),
        halo("lon", lax.rem(p + 1, LONS), 3, col_send.at[1], col_recv.at[1]),
    ]
    halos[0].start()
    halos[1].start()

    q_own, g = b // 2, 2 * (b % 2) + x
    orders = []
    for s in (0, 1):
        r = 2 * g + 1 + s
        for t in (0, 1):
            m = 16 * q_own + r if t == 0 else 16 * q_own + 16 - r
            if s == 1:
                m = jnp.where(g == 3, 16 * q_own + 8 * t, m)
            orders.append(m)
    for copy in tables[:8]:
        copy.wait()
    degree = lax.broadcasted_iota(jnp.int32, (MODES, 128), 0)
    deg = degree.astype(f32)
    cosine, sine_all = small[0:8], small[8:16]
    log_sine = jnp.log(sine_all)
    entry = lax.broadcasted_iota(jnp.int32, (2, 128), 0) * 128 + lax.broadcasted_iota(
        jnp.int32, (2, 128), 1
    )
    diagonals = []
    for mu, m in enumerate(orders):
        order = m.astype(f32)
        order2 = order * order

        def factor(d):
            return jnp.sqrt(
                jnp.maximum(4.0 * d * d - 1.0, 1.0) / jnp.maximum(d * d - order2, 1.0)
            )

        factor_now, factor_prev = factor(deg), factor(deg - 1.0)
        grow[mu] = jnp.where(degree > m, factor_now, 0.0)
        drop[mu] = jnp.where(degree > m + 1, factor_now / factor_prev, 0.0)
        seed[mu] = jnp.where(degree == m, 1.0, 0.0)
        log_start = jnp.where(entry == m, small[48:50], 0.0)
        log_start = jnp.sum(jnp.sum(log_start, axis=1, keepdims=True), axis=0, keepdims=True)
        log_diagonal = log_start + order * log_sine
        diagonals.append(
            jnp.where(
                log_diagonal >= start_floor, jnp.exp(jnp.maximum(log_diagonal, start_floor)), 0.0
            )
        )

    def advance(i, state):
        first = pl.multiple_of(i * 8, 8)
        at = pl.ds(first, 8)
        rows = [(grow[mu, at], drop[mu, at], seed[mu, at]) for mu in range(4)]
        state = list(state)
        for n in range(8):
            row_at = pl.ds(pl.multiple_of((first + n) * 8, 8), 8)
            for mu in range(4):
                a8, q8, d8 = rows[mu]
                latest, before = state[mu]
                step = a8[n : n + 1] * cosine
                rest = d8[n : n + 1] * diagonals[mu] - q8[n : n + 1] * before
                fresh = step * latest + rest
                raw[mu, row_at] = fresh
                state[mu] = (fresh, latest)
        return tuple(state)

    zero = jnp.zeros((8, 128), f32)
    lax.fori_loop(0, MODES // 8, advance, ((zero, zero),) * 4)
    for mu in range(4):
        for s in range(4):
            h, half = s // 2, s % 2
            block = raw[mu, pl.ds(s, MODES, stride=8), :]
            high, low = split(block)
            t_h[2 * mu + h, :, pl.ds(half * 128, 128)] = high
            t_l[2 * mu + h, :, pl.ds(half * 128, 128)] = low
            high, low = split(block.T)
            tt_h[2 * mu + h, pl.ds(half * 128, 128), :] = high
            tt_l[2 * mu + h, pl.ds(half * 128, 128), :] = low

    lane_all = lax.broadcasted_iota(jnp.int32, (MODES, 128), 1)
    mu_lane = (lane_all // 2) % 4
    own = [(mu_lane == mu) & (lane_all // 64 == h) for mu in range(4) for h in (0, 1)]
    own_low = [mask[0:256] for mask in own]

    def by_degree(ratios, first, rows):
        count = ratios.shape[0]
        frequency = lax.broadcasted_iota(jnp.int32, (count, MODES), 0) + first
        last = jnp.zeros((count, MODES), jnp.int32)
        for n in range(first, 5):
            last = jnp.where(frequency == n, cut[n], last)
        kept = lax.broadcasted_iota(jnp.int32, (count, MODES), 1) <= last
        return lax.dot_general(
            jnp.where(kept, ratios[...], 0.0),
            rows,
            (((0,), (0,)), ((), ())),
            precision=lax.Precision.HIGHEST,
            preferred_element_type=f32,
        )

    w_lane = jnp.full((MODES, 128), 2.0, f32)
    for mu, m in enumerate(orders):
        w_lane = jnp.where(mu_lane == mu, jnp.where(m == 0, 1.0, 2.0), w_lane)
    mult[0] = by_degree(real, 0, select[z, 0:5]) * w_lane
    mult[1] = by_degree(imag, 1, select[z, 8:12]) * w_lane

    j_own = 16 * b + 8 * x + lax.broadcasted_iota(jnp.int32, (8, 256), 0)
    term = lax.broadcasted_iota(jnp.int32, (8, 256), 1) + 1
    angle = ((term * (2 * j_own + 1)) & (2 * NLAT - 1)).astype(f32) * (math.pi / NLAT)
    termf = term.astype(f32)
    series = jnp.sum(jnp.cos(angle) / (4.0 * termf * termf - 1.0), axis=1, keepdims=True)
    weight = (2.0 / NLAT) * (1.0 - 2.0 * series) * (2.0 * math.pi / NLON)
    weight = jnp.broadcast_to(weight, (8, 128))

    for g4 in range(4):
        circles[pl.ds(64 * g4 + ROWS, 64 - ROWS)] = jnp.zeros((64 - ROWS, 768), f32)
    circles[pl.ds(0, 192), pl.ds(512, 256)] = jnp.zeros((192, 256), f32)
    circles[pl.ds(192, 64), pl.ds(256, 256)] = jnp.zeros((64, 256), f32)
    place = lambda g4: 2 * (g4 % 2) + g4 // 2
    tw = lambda r: (small[16 + r : 17 + r], small[24 + r : 25 + r])
    for copy in tables[8:]:
        copy.wait()
    drain(r1, LONS, recv_sem.at[0])

    def analyse(i, carry):
        first = pl.multiple_of(i * 8, 8)
        x = [r1[d, pl.ds(first, 8)] for d in range(16)]
        even = {d: x[d] + x[16 - d] for d in range(1, 8)}
        odd = {d: x[d] - x[16 - d] for d in range(1, 8)}
        c, s = sixteen(x[0], x[8], even, odd)
        for r in range(1, 8):
            co, si = tw(r)
            at = pl.ds(64 * place((r - 1) // 2) + first, 8)
            column = 256 * ((r - 1) % 2)
            circles[at, pl.ds(column, 128)] = c[r] * co - s[r] * si
            circles[at, pl.ds(column + 128, 128)] = -s[r] * co - c[r] * si
        at = pl.ds(192 + first, 8)
        circles[at, pl.ds(512, 128)] = c[0]
        circles[at, pl.ds(640, 128)] = c[8]
        return carry

    lax.fori_loop(0, ROWS // 8, analyse, 0)
    found = dot_wide(split(circles[...]), fwd[...])
    lane8 = lax.broadcasted_iota(jnp.int32, (8, 128), 1)
    low_half = lane8 < 64
    granule = [lane8 // 8 == i for i in range(16)]

    def turn(value, granules):
        return pltpu.roll(value, (8 * granules) % 128, 1) if granules % 16 else value

    for half in (0, 1):
        tiles = {}
        for g2 in (0, 1):
            for i in range(6):
                first = 64 * (2 * half + g2) + 8 * i
                tiles[8 * g2 + i] = found[first : first + 8] * weight
        for q in range(16):
            message = jnp.zeros((8, 128), f32)
            for i, tile in tiles.items():
                message = jnp.where(granule[i], turn(tile, i - q), message)
            s2[half, q] = message
    def pass_on(send, recv, index):
        return pltpu.make_async_remote_copy(
            src_ref=send.at[1 - x],
            dst_ref=recv.at[x],
            send_sem=send_sem.at[index],
            recv_sem=recv_sem.at[index],
            device_id={"lon": partner},
            device_id_type=MESH,
        )

    second = pass_on(s2, r2, 1)
    second.start()
    r2[x] = s2[x]
    second.wait_recv()
    for q in range(16):
        one, two = r2[0, q], r2[1, q]
        s3[2 * q] = jnp.where(low_half, one, pltpu.roll(two, 64, 1))
        s3[2 * q + 1] = jnp.where(low_half, pltpu.roll(one, 64, 1), two)
    r3[b] = s3[b]
    exchange("lat", b, LATS, s3, r3, send_sem.at[2], recv_sem.at[2])
    def pack(f, packed):
        packed = list(packed)
        for r in range(RAD):
            x = xv[f, r]
            at = f + 64 * (r % 2)
            here = lane == at
            for side in (0, 1):
                i = 2 * side + r // 2
                packed[i] = jnp.where(here, pltpu.roll(x, lax.rem(at + side, 128), 1), packed[i])
        return tuple(packed)

    packed = lax.fori_loop(0, FIELDS, pack, (jnp.zeros((16, 128), f32),) * 4)
    for i in range(4):
        col_send[i // 2, i % 2] = packed[i]
    halos[2].start()
    halos[3].start()

    drain(r3, LATS, recv_sem.at[2])

    wide = jnp.concatenate(split(r3[...].reshape(256, 128)), axis=1)
    degrees = jnp.zeros((MODES, 128), f32)
    for i in range(8):
        degrees = jnp.where(own[i], dot_wide((t_h[i], t_l[i]), wide), degrees)
    degrees = degrees + pltpu.roll(degrees, 64, 1)
    swapped = jnp.where(
        (lane_all // 8) % 2 == 0, pltpu.roll(degrees, 120, 1), pltpu.roll(degrees, 8, 1)
    )
    bent = mult[0] * degrees + mult[1] * swapped
    wide = jnp.concatenate(split(bent), axis=1)
    rows_out = jnp.zeros((256, 128), f32)
    for i in range(8):
        rows_out = jnp.where(own_low[i], dot_wide((tt_h[i], tt_l[i]), wide), rows_out)
    s4[...] = rows_out.reshape(32, 8, 128)
    r4[b] = s4[b]
    exchange("lat", b, LATS, s4, r4, send_sem.at[3], recv_sem.at[3])
    for i in (2, 3, 0, 1):
        halos[i].wait_recv()
    band = (16 * b + row).astype(f32)
    sine = jnp.sin((band + 0.5) * (math.pi / NLAT))
    half_sine = 0.5 * sine
    south_keep = jnp.where(b == LATS - 1, 0.0, 1.0)
    north_keep = jnp.where(b == 0, 0.0, 1.0)
    jl = [[jlat[v, w] for w in range(VARS)] for v in range(VARS)]
    jo = [[jlon[v, w] for w in range(VARS)] for v in range(VARS)]
    jr = [[jrad[v, w] for w in range(VARS)] for v in range(VARS)]

    def one_instance(t, carry):
        for r in range(RAD):
            lat_d, rad_d, lon_d, rest = [], [], [], []
            for w in range(VARS):
                f = w * INST + t
                x = xv[f, r]
                index = f * RAD + r
                at = f + 64 * (r % 2)
                south_row = row_recv[0, pl.ds(index, 1)] * south_keep
                north_row = row_recv[1, pl.ds(index, 1)] * north_keep
                south = jnp.where(row == 15, south_row, pltpu.roll(x, 15, 0))
                north = jnp.where(row == 0, north_row, pltpu.roll(x, 1, 0))
                east_col = pltpu.roll(col_recv[0, r // 2], 127 - at, 1)
                west_col = pltpu.roll(col_recv[1, r // 2], lax.rem(128 - at, 128), 1)
                east = jnp.where(lane == 127, east_col, pltpu.roll(x, 127, 1))
                west = jnp.where(lane == 0, west_col, pltpu.roll(x, 1, 1))
                above = xv[f, r + 1] if r < RAD - 1 else x
                below = xv[f, r - 1] if r > 0 else jnp.zeros_like(x)
                lat_d.append(half_sine * (south - north))
                rad_d.append(half_sine * (above - below))
                lon_d.append(0.5 * (east - west))
                spread = half_sine * (south + north + above + below - 4.0 * x)
                timing = -spread - 0.5 * (east + west - 2.0 * x)
                for lag in range(1, 5):
                    back = xv[w * INST + lax.rem(t + 9 - lag, 9), r]
                    ahead = xv[w * INST + lax.rem(t + lag, 9), r]
                    timing = timing + SPECTRAL[lag - 1] * (back - ahead)
                rest.append(timing)
            for v in range(VARS):
                total = rest[v]
                for w in range(VARS):
                    total = total + (
                        jl[v][w] * lat_d[w] + jr[v][w] * rad_d[w] + jo[v][w] * lon_d[w]
                    )
                base[v * INST + t, r] = total
        return carry

    lax.fori_loop(0, INST, one_instance, 0)
    put_base = pltpu.make_async_copy(base, base_hbm, local.at[0])
    put_base.start()

    drain(r4, LATS, recv_sem.at[3])

    for q in range(16):
        one, two = r4[2 * q], r4[2 * q + 1]
        s5[0, q] = jnp.where(low_half, one, pltpu.roll(two, 64, 1))
        s5[1, q] = jnp.where(low_half, pltpu.roll(one, 64, 1), two)
    fifth = pass_on(s5, r5, 4)
    fifth.start()
    r5[x] = s5[x]
    fifth.wait_recv()

    blocks = []
    for half in (0, 1):
        messages = [r5[half, q] for q in range(16)]
        for g2 in (0, 1):
            for i in range(6):
                tile = turn(messages[0], -(8 * g2 + i))
                for q in range(1, 16):
                    tile = jnp.where(granule[q], turn(messages[q], q - 8 * g2 - i), tile)
                blocks.append(tile)
            blocks.append(jnp.zeros((16, 128), f32))
    found = split(jnp.concatenate(blocks, axis=0))
    lines[...] = dot(jnp.concatenate(found, axis=1), inv[0:256]) + dot(found[0], inv[256:384])

    def synthesise(i, carry):
        first = pl.multiple_of(i * 8, 8)
        even, odd = {}, {}
        for r in range(1, 8):
            co, si = tw(r)
            at = pl.ds(64 * place((r - 1) // 2) + first, 8)
            column = 256 * ((r - 1) % 2)
            re, im = lines[at, pl.ds(column, 128)], lines[at, pl.ds(column + 128, 128)]
            even[r] = re * co - im * si
            odd[r] = re * si + im * co
        at = pl.ds(192 + first, 8)
        c, s = sixteen(lines[at, pl.ds(512, 128)], lines[at, pl.ds(640, 128)], even, odd)
        s6[0, pl.ds(first, 8)] = c[0]
        s6[8, pl.ds(first, 8)] = c[8]
        for d in range(1, 8):
            s6[d, pl.ds(first, 8)] = c[d] - s[d]
            s6[16 - d, pl.ds(first, 8)] = c[d] + s[d]
        return carry

    lax.fori_loop(0, ROWS // 8, synthesise, 0)
    keep = pltpu.make_async_copy(s6.at[p], normal_hbm.at[p], local.at[1])
    keep.start()
    exchange("lon", p, LONS, s6, normal_hbm, send_sem.at[5], recv_sem.at[5])
    for i, (buffer, count) in enumerate([(s1, LONS), (s3, LATS), (s4, LATS), (s6, LONS)]):
        drain(buffer, count, send_sem.at[(0, 2, 3, 5)[i]])
    second.wait_send()
    fifth.wait_send()
    for copy in halos:
        copy.wait_send()
    put_base.wait()
    keep.wait()
    drain(normal_hbm, LONS, recv_sem.at[5])


def finish(base_hbm, circles_hbm, jrad, out_hbm, normal, circles, base, sem):
    b = lax.axis_index("lat")
    get_circles = pltpu.make_async_copy(circles_hbm, circles, sem.at[0])
    get_circles.start()
    part = lambda v: pl.ds(v * INST, INST)
    gets = [
        pltpu.make_async_copy(base_hbm.at[part(v)], base.at[part(v)], sem.at[1 + v])
        for v in range(VARS)
    ]
    for copy in gets:
        copy.start()
    jr = [[jrad[v, w] for w in range(VARS)] for v in range(VARS)]
    row = lax.broadcasted_iota(jnp.int32, (8, 128), 0)
    get_circles.wait()
    for h in (0, 1):
        band = (16 * b + 8 * h + row).astype(f32)
        half_sine = 0.5 * jnp.sin((band + 0.5) * (math.pi / NLAT))
        rows = pl.ds(8 * h, 8)
        n = {}
        for v in range(VARS):
            value = {}
            for k in range(5):
                for kind in (0, 1) if k else (0,):
                    z, i = PLACE[v, k, kind]
                    value[k, kind] = circles[2 * z + h, pl.ds(8 * i, 8)]
            even = {k: value[k, 0] for k in range(1, 5)}
            odd = {k: value[k, 1] for k in range(1, 5)}
            c, s = fold_time(value[0, 0], even, odd)
            n[v, 0] = value[0, 0] + sum(even.values())
            for t in range(1, 5):
                n[v, t], n[v, 9 - t] = c[t] + s[t], c[t] - s[t]
        for v in range(VARS):
            for t in range(INST):
                normal[v * INST + t, rows] = n[v, t]
        for v in range(VARS):
            if h == 0:
                gets[v].wait()
            for t in range(INST):
                total = -n[v, t]
                for w in range(VARS):
                    total = total + jr[v][w] * n[w, t]
                at = v * INST + t
                base[at, 3, rows] = base[at, 3, rows] + half_sine * total
    puts = [
        pltpu.make_async_copy(base.at[part(v)], out_hbm.at[part(v)], sem.at[1 + v])
        for v in range(VARS)
    ]
    for copy in puts:
        copy.start()
    for copy in puts:
        copy.wait()


def shards(flow_state, jacobian_lat, jacobian_lon, jacobian_rad, ratio_real, ratio_imag, cut):
    x = flow_state.reshape(FIELDS, RAD, 16, 128)
    table = circle_table()
    small = np.zeros((56, 128), np.float32)
    small[0:16] = latitude_rows()
    small[16:32] = twiddle_table()
    small[48:50] = start_logs().reshape(2, 128)
    high, low = split_table(table)
    constants = [
        np.concatenate([np.ascontiguousarray(high.T), np.ascontiguousarray(low.T)], axis=1),
        np.concatenate([high, high, low]),
        small,
        ratio_rows().astype(np.float32),
    ]
    constants = [jnp.asarray(part) for part in constants]
    smem = pl.BlockSpec(memory_space=pltpu.SMEM)
    vmem = pl.BlockSpec(memory_space=pltpu.VMEM)
    hbm = pl.BlockSpec(memory_space=pl.ANY)
    v = lambda *shape: pltpu.VMEM(shape, f32)
    w = lambda *shape: pltpu.VMEM(shape, bf16)
    base, circles = pl.pallas_call(
        far_field,
        out_shape=[
            jax.ShapeDtypeStruct((FIELDS, RAD, 16, 128), f32),
            jax.ShapeDtypeStruct((16, ROWS, 128), f32),
        ],
        in_specs=[pl.BlockSpec(memory_space=pltpu.HBM)] * (7 + len(constants)),
        out_specs=[hbm, hbm],
        scratch_shapes=[
            v(FIELDS, 16, 128), v(FIELDS, RAD, 16, 128), v(FIELDS, RAD, 16, 128),
            v(16, ROWS, 128), v(16, ROWS, 128),
            v(2, 16, 8, 128), v(2, 16, 8, 128),
            v(32, 8, 128), v(32, 8, 128),
            v(32, 8, 128), v(32, 8, 128),
            v(2, 16, 8, 128), v(2, 16, 8, 128),
            v(16, ROWS, 128),
            v(2, 180, 128), v(2, 180, 128), v(2, 2, 16, 128), v(2, 2, 16, 128),
            v(256, 768), v(256, 768), v(4, MODES * 8, 128),
            w(8, 256, 256), w(8, 256, 256), w(8, 256, 256), w(8, 256, 256),
            v(4, MODES, 128), v(4, MODES, 128), v(4, MODES, 128), v(2, MODES, 128),
            w(768, 256), w(384, 768), v(56, 128), v(8, 16, 128),
            pltpu.SMEM((5, 5), f32), pltpu.SMEM((5, 5), f32), pltpu.SMEM((5, 5), f32),
            pltpu.SMEM((5,), jnp.int32), v(5, MODES), v(4, MODES),
            pltpu.SemaphoreType.DMA((6,)), pltpu.SemaphoreType.DMA((6,)),
            pltpu.SemaphoreType.DMA((4,)), pltpu.SemaphoreType.DMA((4,)),
            pltpu.SemaphoreType.DMA((12,)),
        ],
        compiler_params=pltpu.CompilerParams(
            collective_id=0, has_side_effects=True, vmem_limit_bytes=62 * 1024 * 1024
        ),
        name="far_field",
    )(x, jacobian_lat, jacobian_lon, jacobian_rad, cut, ratio_real.T, ratio_imag.T,
      *constants)
    residual, normal = pl.pallas_call(
        finish,
        out_shape=[
            jax.ShapeDtypeStruct((FIELDS, RAD, 16, 128), f32),
            jax.ShapeDtypeStruct((FIELDS, 16, 128), f32),
        ],
        in_specs=[hbm, hbm, smem],
        out_specs=[hbm, vmem],
        scratch_shapes=[
            v(16, ROWS, 128), v(FIELDS, RAD, 16, 128), pltpu.SemaphoreType.DMA((6,))
        ],
        compiler_params=pltpu.CompilerParams(vmem_limit_bytes=62 * 1024 * 1024),
        name="finish",
    )(base, circles, jacobian_rad)
    return (
        residual.reshape(VARS, INST, RAD, 16, 128),
        normal.reshape(VARS, INST, 16, 128),
    )


def solution(mesh):
    placed = (P(None, None, None, "lat", "lon"), P(), P(), P(), P(), P(), P())
    return jax.shard_map(
        shards,
        mesh=mesh,
        in_specs=placed,
        out_specs=(P(None, None, None, "lat", "lon"), P(None, None, "lat", "lon")),
        check_vma=False,
    )
```

time: 92.7 us -> 66.6 us (0.72)
  the two profiles are of different devices: /device:TPU:2 before, /device:TPU:1 now
where the time goes in v2:
time: 66.6 us; the launch traced here: 66.2 us
  Pallas kernels  65.6 us (98%)
    pallas_call x1, Pallas kernels, shards(): pl.pallas_call(far_field, out_shape=[jax.ShapeDtypeStruct((FIELDS, RAD, 1...  61.4 us
    pallas_call x1, Pallas kernels, shards(): pl.pallas_call(finish, out_shape=[jax.ShapeDtypeStruct((FIELDS, RAD, 16,...  4.21 us

profile of v2, /device:TPU:1, one launch (start us, length us, event | category | flops | bytes accessed | tf_op | source)
XLA Modules:
  0.0 66.2 jit_solution(2279459143914091970)
XLA Ops:
  0.6 61.4 %far_field.1 = (f32[45,4,16,128]{3,2,1,0:T(8,128)}, f32[16,48,128]{2,1,0:T(8,128)}) custom-call(f32[45,4,16,128]{3,2,1,0:T(8,128)} %bitcast.5, f32[5,5]{1,0:T(8,128)} %jlat_hbm.1, f32[5,5]{1,0:T(8,128)} %jlon_hbm.1, f32[5,5]{1,0:T(8,128)} %jrad.1, s32[5]{0:T(128)} %cut_hbm.1, f32[5,256]{1,0:T(8,128)} %bitcast.6, f32[4,256]{1,0:T(4,128)} %bitcast.7, ...), custom_call_target="tpu_custom_call" | custom-call | tf_op jit(solution)/shard_map/far_field/pallas_call | solution.py:670
  62.0 4.2 %finish.1 = (f32[45,4,16,128]{3,2,1,0:T(8,128)}, f32[45,16,128]{2,1,0:T(8,128)}) custom-call(f32[45,4,16,128]{3,2,1,0:T(8,128)} %get-tuple-element.6.base_hbm, f32[16,48,128]{2,1,0:T(8,128)} %get-tuple-element.7.circles_hbm, f32[5,5]{1,0:T(8,128)} %jrad.1), custom_call_target="tpu_custom_call" | custom-call | tf_op jit(solution)/shard_map/finish/pallas_call | solution.py:703

commit v3 on v2

--- a/solution.py
+++ b/solution.py
@@ -12,7 +12,7 @@
 
 VARS, INST, RAD, NLAT, NLON, MODES = 5, 9, 4, 512, 2048, 256
 FIELDS = VARS * INST
-ROWS = 48
+ROWS = 64
 LATS, LONS = 32, 16
 MESH = pl.DeviceIdType.MESH
 f32, bf16 = jnp.float32, jnp.bfloat16
@@ -55,27 +55,32 @@
     return np.concatenate([np.cos(angle), np.sin(angle)])
 
 
+FOUR, THREE = (0, 5, 8, 13), (2, 3, 7, 10, 15)
+
+
 def slot_table():
     pairs = [[(v, n, 0), (v, n, 1)] for v in range(VARS) for n in range(1, 5)]
-    pairs += [[(0, 0, 0), (1, 0, 0)], [(2, 0, 0), (3, 0, 0)], [(4, 0, 0), None], [None, None]]
-    return [sum(pairs[3 * z : 3 * z + 3], []) for z in range(8)]
+    singles = [[(v, 0, 0)] for v in range(VARS)]
+    slots = [pairs.pop() for _ in range(LONS)]
+    for p in FOUR:
+        slots[p] = slots[p] + pairs.pop()
+    for p in THREE:
+        slots[p] = slots[p] + singles.pop()
+    return slots
 
 
 SLOTS = slot_table()
-PLACE = {item: (z, i) for z in range(8) for i, item in enumerate(SLOTS[z]) if item}
+PLACE = {item: (p, i) for p in range(LONS) for i, item in enumerate(SLOTS[p])}
 
 
 def ratio_rows():
-    rows = np.zeros((8, 16, 2, 8, 8))
-    for z in range(8):
-        for i, item in enumerate(SLOTS[z]):
-            if item is None:
-                continue
-            _, n, part = item
-            rows[z, n, :, i] = 2 / 9 if n else 1 / 9
+    rows = np.zeros((LONS, 16, 2, 4, 16))
+    for p in range(LONS):
+        for i, (_, n, part) in enumerate(SLOTS[p]):
+            rows[p, n, :, i] = 2 / 9 if n else 1 / 9
             if n:
-                rows[z, 7 + n, :, i] = -2 / 9 if part else 2 / 9
-    return rows.reshape(8, 16, 128)
+                rows[p, 7 + n, :, i] = -2 / 9 if part else 2 / 9
+    return rows.reshape(LONS, 16, 128)
 
 
 def fold_time(first, even, odd):
@@ -89,9 +94,8 @@
 
 def latitude_rows():
     column = np.arange(256)
-    j = np.stack([16 * (column // 8) + 8 * h + column % 8 for h in (0, 1)])
-    angle = (j.reshape(4, 128) + 0.5) * np.pi / NLAT
-    angle = np.concatenate([angle, angle])
+    angle = (16 * (column // 8) + column % 8 + 0.5) * np.pi / NLAT
+    angle = np.tile(angle.reshape(2, 128), (4, 1))
     return np.concatenate([np.cos(angle), np.sin(angle)])
 
 
@@ -165,12 +169,14 @@
     return c, s
 
 
-def exchange(axis, me, count, send, recv, send_sem, recv_sem):
+def exchange(axis, me, count, send, recv, send_sem, recv_sem, rows=None):
+    part = (lambda ref, i: ref.at[i]) if rows is None else (lambda ref, i: ref.at[i, rows])
+
     def one(step, carry):
         peer = lax.rem(me + step, count)
         pltpu.make_async_remote_copy(
-            src_ref=send.at[peer],
-            dst_ref=recv.at[me],
+            src_ref=part(send, peer),
+            dst_ref=part(recv, me),
             send_sem=send_sem,
             recv_sem=recv_sem,
             device_id={axis: peer},
@@ -181,15 +187,26 @@
     lax.fori_loop(1, count, one, 0)
 
 
-def drain(buffer, count, sem):
+def drain(buffer, count, sem, rows=None):
     part = buffer.at[pl.ds(0, count - 1)]
+    if rows is not None:
+        part = buffer.at[pl.ds(0, count - 1), pl.ds(0, rows)]
     pltpu.make_async_copy(part, part, sem).wait()
+
+
+def mirrored(value):
+    row = lax.broadcasted_iota(jnp.int32, (8, 128), 0)
+    value = pltpu.roll(value, 4, 0)
+    for bit in (2, 1):
+        up, down = pltpu.roll(value, 8 - bit, 0), pltpu.roll(value, bit, 0)
+        value = jnp.where((row & bit) == 0, up, down)
+    return value
 
 
 def far_field(
     x_hbm, jlat_hbm, jlon_hbm, jrad_hbm, cut_hbm, real_hbm, imag_hbm, fwd_hbm, inv_hbm, small_hbm,
     select_hbm, base_hbm, normal_hbm,
-    shell, xv, base, s1, r1, s2, r2, s3, r3, s4, r4, s5, r5, s6,
+    shell, xv, base, s1, r1, s3, r3, s4, r4, s6,
     row_send, row_recv, col_send, col_recv,
     circles, lines, raw, t_h, t_l, tt_h, tt_l, grow, drop, seed, mult,
     fwd, inv, small, select, jlat, jlon, jrad, cut, real, imag,
@@ -197,9 +214,15 @@
 ):
     b = lax.axis_index("lat")
     p = lax.axis_index("lon")
-    z, x = p // 2, p % 2
-    partner = p + 1 - 2 * x
-
+    among = lambda group: functools.reduce(lambda a, c: a | c, [p == i for i in group])
+    four, three = among(FOUR), among(THREE)
+    two = jnp.logical_not(four | three)
+    lower, upper, middle = pl.ds(0, 32), pl.ds(32, 32), pl.ds(32, 16)
+
+    get_shell = pltpu.make_async_copy(x_hbm.at[:, 3], shell, local.at[0])
+    get_shell.start()
+    for d in range(LONS):
+        r1[d, upper] = jnp.zeros((32, 128), f32)
     barrier = pltpu.get_barrier_semaphore()
 
     def greet(axis, me, count):
@@ -214,9 +237,7 @@
     greet("lon", p, LONS)
     greet("lat", b, LATS)
 
-    get_shell = pltpu.make_async_copy(x_hbm.at[:, 3], shell, local.at[0])
     get_all = pltpu.make_async_copy(x_hbm, xv, local.at[1])
-    get_shell.start()
     get_all.start()
     pairs = [
         (small_hbm, small), (real_hbm, real), (imag_hbm, imag), (cut_hbm, cut),
@@ -230,26 +251,38 @@
         copy.start()
 
     get_shell.wait()
-    for z8 in range(8):
-        for i, item in enumerate(SLOTS[z8]):
-            if item is None:
-                for h in (0, 1):
-                    s1[2 * z8 + h, pl.ds(8 * i, 8)] = jnp.zeros((8, 128), f32)
+    for d in range(LONS):
+        for i in range(len(SLOTS[d]), 4):
+            s1[d, pl.ds(16 * i, 16)] = jnp.zeros((16, 128), f32)
     for v in range(VARS):
-        for h in (0, 1):
-            q = [shell[v * INST + t, pl.ds(8 * h, 8)] for t in range(INST)]
-            even = {k: q[k] + q[9 - k] for k in range(1, 5)}
-            odd = {k: q[k] - q[9 - k] for k in range(1, 5)}
-            c, s = fold_time(q[0], even, odd)
-            parts = {(v, 0, 0): q[0] + sum(even.values())}
-            for n in range(1, 5):
-                parts[v, n, 0], parts[v, n, 1] = c[n], s[n]
-            for item, value in parts.items():
-                z8, i = PLACE[item]
-                s1[2 * z8 + h, pl.ds(8 * i, 8)] = value
+        q = [shell[v * INST + t] for t in range(INST)]
+        even = {k: q[k] + q[9 - k] for k in range(1, 5)}
+        odd = {k: q[k] - q[9 - k] for k in range(1, 5)}
+        c, s = fold_time(q[0], even, odd)
+        parts = {(v, 0, 0): q[0] + sum(even.values())}
+        for n in range(1, 5):
+            parts[v, n, 0], parts[v, n, 1] = c[n], s[n]
+        for item, value in parts.items():
+            d, i = PLACE[item]
+            s1[d, pl.ds(16 * i, 16)] = value
     r1[p] = s1[p]
     pl.semaphore_wait(barrier, LONS + LATS - 2)
-    exchange("lon", p, LONS, s1, r1, send_sem.at[0], recv_sem.at[0])
+    for group, rows in ((FOUR, upper), (THREE, middle)):
+        for peer in group:
+
+            @pl.when(p != peer)
+            def _():
+                pltpu.make_async_remote_copy(
+                    src_ref=s1.at[peer, rows],
+                    dst_ref=r1.at[p, rows],
+                    send_sem=send_sem.at[1],
+                    recv_sem=recv_sem.at[1],
+                    device_id={"lon": peer},
+                    device_id_type=MESH,
+                ).start()
+
+
+    exchange("lon", p, LONS, s1, r1, send_sem.at[0], recv_sem.at[0], lower)
 
     get_all.wait()
     lane = lax.broadcasted_iota(jnp.int32, (16, 128), 1)
@@ -277,16 +310,18 @@
     halos[0].start()
     halos[1].start()
 
-    q_own, g = b // 2, 2 * (b % 2) + x
+    q_own = b // 2
     orders = []
-    for s in (0, 1):
-        r = 2 * g + 1 + s
-        for t in (0, 1):
-            m = 16 * q_own + r if t == 0 else 16 * q_own + 16 - r
-            if s == 1:
-                m = jnp.where(g == 3, 16 * q_own + 8 * t, m)
-            orders.append(m)
-    for copy in tables[:8]:
+    for low in (0, 1):
+        g = 2 * (b % 2) + low
+        for s in (0, 1):
+            r = 2 * g + 1 + s
+            for t in (0, 1):
+                m = 16 * q_own + r if t == 0 else 16 * q_own + 16 - r
+                if s == 1:
+                    m = jnp.where(g == 3, 16 * q_own + 8 * t, m)
+                orders.append(m)
+    for copy in tables:
         copy.wait()
     degree = lax.broadcasted_iota(jnp.int32, (MODES, 128), 0)
     deg = degree.astype(f32)
@@ -321,11 +356,11 @@
     def advance(i, state):
         first = pl.multiple_of(i * 8, 8)
         at = pl.ds(first, 8)
-        rows = [(grow[mu, at], drop[mu, at], seed[mu, at]) for mu in range(4)]
+        rows = [(grow[mu, at], drop[mu, at], seed[mu, at]) for mu in range(8)]
         state = list(state)
         for n in range(8):
             row_at = pl.ds(pl.multiple_of((first + n) * 8, 8), 8)
-            for mu in range(4):
+            for mu in range(8):
                 a8, q8, d8 = rows[mu]
                 latest, before = state[mu]
                 step = a8[n : n + 1] * cosine
@@ -336,22 +371,26 @@
         return tuple(state)
 
     zero = jnp.zeros((8, 128), f32)
-    lax.fori_loop(0, MODES // 8, advance, ((zero, zero),) * 4)
-    for mu in range(4):
-        for s in range(4):
-            h, half = s // 2, s % 2
-            block = raw[mu, pl.ds(s, MODES, stride=8), :]
+    lax.fori_loop(0, MODES // 8, advance, ((zero, zero),) * 8)
+    for mu in range(8):
+        for half in range(2):
+            block = raw[mu, pl.ds(half, MODES, stride=8), :]
             high, low = split(block)
-            t_h[2 * mu + h, :, pl.ds(half * 128, 128)] = high
-            t_l[2 * mu + h, :, pl.ds(half * 128, 128)] = low
+            t_h[mu, :, pl.ds(half * 128, 128)] = high
+            t_l[mu, :, pl.ds(half * 128, 128)] = low
             high, low = split(block.T)
-            tt_h[2 * mu + h, pl.ds(half * 128, 128), :] = high
-            tt_l[2 * mu + h, pl.ds(half * 128, 128), :] = low
+            tt_h[mu, pl.ds(half * 128, 128), :] = high
+            tt_l[mu, pl.ds(half * 128, 128), :] = low
 
     lane_all = lax.broadcasted_iota(jnp.int32, (MODES, 128), 1)
-    mu_lane = (lane_all // 2) % 4
-    own = [(mu_lane == mu) & (lane_all // 64 == h) for mu in range(4) for h in (0, 1)]
-    own_low = [mask[0:256] for mask in own]
+    mu_lane = (lane_all // 2) % 8
+    own = [mu_lane == mu for mu in range(8)]
+    m_lane = jnp.zeros((MODES, 128), jnp.int32)
+    for mu, m in enumerate(orders):
+        m_lane = jnp.where(own[mu], m, m_lane)
+    odd_lane = ((degree + m_lane) & 1 == 1) & (lane_all >= 64)
+    mult[2] = jnp.where(odd_lane, -1.0, 1.0)
+    w_lane = jnp.where(m_lane == 0, 1.0, 2.0) * mult[2]
 
     def by_degree(ratios, first, rows):
         count = ratios.shape[0]
@@ -368,29 +407,30 @@
             preferred_element_type=f32,
         )
 
-    w_lane = jnp.full((MODES, 128), 2.0, f32)
-    for mu, m in enumerate(orders):
-        w_lane = jnp.where(mu_lane == mu, jnp.where(m == 0, 1.0, 2.0), w_lane)
-    mult[0] = by_degree(real, 0, select[z, 0:5]) * w_lane
-    mult[1] = by_degree(imag, 1, select[z, 8:12]) * w_lane
-
-    j_own = 16 * b + 8 * x + lax.broadcasted_iota(jnp.int32, (8, 256), 0)
-    term = lax.broadcasted_iota(jnp.int32, (8, 256), 1) + 1
+    mult[0] = by_degree(real, 0, select[p, 0:5]) * w_lane
+    mult[1] = by_degree(imag, 1, select[p, 8:12]) * w_lane
+
+    j_own = 16 * b + lax.broadcasted_iota(jnp.int32, (16, 256), 0)
+    term = lax.broadcasted_iota(jnp.int32, (16, 256), 1) + 1
     angle = ((term * (2 * j_own + 1)) & (2 * NLAT - 1)).astype(f32) * (math.pi / NLAT)
     termf = term.astype(f32)
     series = jnp.sum(jnp.cos(angle) / (4.0 * termf * termf - 1.0), axis=1, keepdims=True)
     weight = (2.0 / NLAT) * (1.0 - 2.0 * series) * (2.0 * math.pi / NLON)
-    weight = jnp.broadcast_to(weight, (8, 128))
-
-    for g4 in range(4):
-        circles[pl.ds(64 * g4 + ROWS, 64 - ROWS)] = jnp.zeros((64 - ROWS, 768), f32)
+    weight = jnp.broadcast_to(weight, (16, 128))
+
     circles[pl.ds(0, 192), pl.ds(512, 256)] = jnp.zeros((192, 256), f32)
     circles[pl.ds(192, 64), pl.ds(256, 256)] = jnp.zeros((64, 256), f32)
-    place = lambda g4: 2 * (g4 % 2) + g4 // 2
     tw = lambda r: (small[16 + r : 17 + r], small[24 + r : 25 + r])
-    for copy in tables[8:]:
-        copy.wait()
-    drain(r1, LONS, recv_sem.at[0])
+    drain(r1, LONS, recv_sem.at[0], 32)
+
+    @pl.when(four)
+    def _():
+        drain(r1, LONS, recv_sem.at[1], 32)
+
+    @pl.when(three)
+    def _():
+        drain(r1, LONS, recv_sem.at[1], 16)
+
 
     def analyse(i, carry):
         first = pl.multiple_of(i * 8, 8)
@@ -400,7 +440,7 @@
         c, s = sixteen(x[0], x[8], even, odd)
         for r in range(1, 8):
             co, si = tw(r)
-            at = pl.ds(64 * place((r - 1) // 2) + first, 8)
+            at = pl.ds(64 * ((r - 1) // 2) + first, 8)
             column = 256 * ((r - 1) % 2)
             circles[at, pl.ds(column, 128)] = c[r] * co - s[r] * si
             circles[at, pl.ds(column + 128, 128)] = -s[r] * co - c[r] * si
@@ -418,35 +458,18 @@
     def turn(value, granules):
         return pltpu.roll(value, (8 * granules) % 128, 1) if granules % 16 else value
 
-    for half in (0, 1):
-        tiles = {}
-        for g2 in (0, 1):
-            for i in range(6):
-                first = 64 * (2 * half + g2) + 8 * i
-                tiles[8 * g2 + i] = found[first : first + 8] * weight
+    for side in (0, 1):
+        tiles = []
+        for h in (0, 1):
+            for i in range(4):
+                for low in (0, 1):
+                    first = 64 * (2 * side + low) + 16 * i + 8 * h
+                    tiles.append(found[first : first + 8] * weight[8 * h : 8 * h + 8])
         for q in range(16):
-            message = jnp.zeros((8, 128), f32)
-            for i, tile in tiles.items():
-                message = jnp.where(granule[i], turn(tile, i - q), message)
-            s2[half, q] = message
-    def pass_on(send, recv, index):
-        return pltpu.make_async_remote_copy(
-            src_ref=send.at[1 - x],
-            dst_ref=recv.at[x],
-            send_sem=send_sem.at[index],
-            recv_sem=recv_sem.at[index],
-            device_id={"lon": partner},
-            device_id_type=MESH,
-        )
-
-    second = pass_on(s2, r2, 1)
-    second.start()
-    r2[x] = s2[x]
-    second.wait_recv()
-    for q in range(16):
-        one, two = r2[0, q], r2[1, q]
-        s3[2 * q] = jnp.where(low_half, one, pltpu.roll(two, 64, 1))
-        s3[2 * q + 1] = jnp.where(low_half, pltpu.roll(one, 64, 1), two)
+            message = turn(tiles[0], -q)
+            for i in range(1, 16):
+                message = jnp.where(granule[i], turn(tiles[i], i - q), message)
+            s3[2 * q + side] = message
     r3[b] = s3[b]
     exchange("lat", b, LATS, s3, r3, send_sem.at[2], recv_sem.at[2])
     def pack(f, packed):
@@ -468,22 +491,73 @@
 
     drain(r3, LATS, recv_sem.at[2])
 
-    wide = jnp.concatenate(split(r3[...].reshape(256, 128)), axis=1)
+    folded = [jnp.where(low_half, r3[i], mirrored(r3[LATS - 1 - i])) for i in range(LATS)]
+    wide = jnp.concatenate(split(jnp.concatenate(folded, axis=0)), axis=1)
     degrees = jnp.zeros((MODES, 128), f32)
     for i in range(8):
         degrees = jnp.where(own[i], dot_wide((t_h[i], t_l[i]), wide), degrees)
+    degrees = degrees * mult[2]
     degrees = degrees + pltpu.roll(degrees, 64, 1)
     swapped = jnp.where(
-        (lane_all // 8) % 2 == 0, pltpu.roll(degrees, 120, 1), pltpu.roll(degrees, 8, 1)
+        (lane_all // 16) % 2 == 0, pltpu.roll(degrees, 112, 1), pltpu.roll(degrees, 16, 1)
     )
     bent = mult[0] * degrees + mult[1] * swapped
     wide = jnp.concatenate(split(bent), axis=1)
     rows_out = jnp.zeros((256, 128), f32)
     for i in range(8):
-        rows_out = jnp.where(own_low[i], dot_wide((tt_h[i], tt_l[i]), wide), rows_out)
-    s4[...] = rows_out.reshape(32, 8, 128)
+        rows_out = jnp.where(own[i], dot_wide((tt_h[i], tt_l[i]), wide), rows_out)
+    for i in range(LATS):
+        here, there = rows_out[8 * i : 8 * i + 8], rows_out[248 - 8 * i : 256 - 8 * i]
+        s4[i] = jnp.where(low_half, here, mirrored(there))
     r4[b] = s4[b]
     exchange("lat", b, LATS, s4, r4, send_sem.at[3], recv_sem.at[3])
+    drain(r4, LATS, recv_sem.at[3])
+
+    blocks = []
+    for g in range(4):
+        messages = [r4[2 * q + g // 2] for q in range(16)]
+        for i in range(4):
+            for h in (0, 1):
+                at = 8 * h + 2 * i + g % 2
+                tile = turn(messages[0], -at)
+                for q in range(1, 16):
+                    tile = jnp.where(granule[q], turn(messages[q], q - at), tile)
+                blocks.append(tile)
+    found = split(jnp.concatenate(blocks, axis=0))
+    lines[...] = dot(jnp.concatenate(found, axis=1), inv[0:256]) + dot(found[0], inv[256:384])
+
+    def synthesise(i, carry):
+        first = pl.multiple_of(i * 8, 8)
+        even, odd = {}, {}
+        for r in range(1, 8):
+            co, si = tw(r)
+            at = pl.ds(64 * ((r - 1) // 2) + first, 8)
+            column = 256 * ((r - 1) % 2)
+            re, im = lines[at, pl.ds(column, 128)], lines[at, pl.ds(column + 128, 128)]
+            even[r] = re * co - im * si
+            odd[r] = re * si + im * co
+        at = pl.ds(192 + first, 8)
+        c, s = sixteen(lines[at, pl.ds(512, 128)], lines[at, pl.ds(640, 128)], even, odd)
+        s6[0, pl.ds(first, 8)] = c[0]
+        s6[8, pl.ds(first, 8)] = c[8]
+        for d in range(1, 8):
+            s6[d, pl.ds(first, 8)] = c[d] - s[d]
+            s6[16 - d, pl.ds(first, 8)] = c[d] + s[d]
+        return carry
+
+    lax.fori_loop(0, ROWS // 8, synthesise, 0)
+    keep = pltpu.make_async_copy(s6.at[p], normal_hbm.at[p], local.at[1])
+    keep.start()
+    parts = ((four, upper), (three, middle), (None, lower))
+    for kind, rows in parts:
+        send = lambda: exchange(
+            "lon", p, LONS, s6, normal_hbm,
+            send_sem.at[4 if kind is None else 5], recv_sem.at[4 if kind is None else 5], rows,
+        )
+        if kind is None:
+            send()
+        else:
+            pl.when(kind)(send)
     for i in (2, 3, 0, 1):
         halos[i].wait_recv()
     band = (16 * b + row).astype(f32)
@@ -536,65 +610,27 @@
     put_base = pltpu.make_async_copy(base, base_hbm, local.at[0])
     put_base.start()
 
-    drain(r4, LATS, recv_sem.at[3])
-
-    for q in range(16):
-        one, two = r4[2 * q], r4[2 * q + 1]
-        s5[0, q] = jnp.where(low_half, one, pltpu.roll(two, 64, 1))
-        s5[1, q] = jnp.where(low_half, pltpu.roll(one, 64, 1), two)
-    fifth = pass_on(s5, r5, 4)
-    fifth.start()
-    r5[x] = s5[x]
-    fifth.wait_recv()
-
-    blocks = []
-    for half in (0, 1):
-        messages = [r5[half, q] for q in range(16)]
-        for g2 in (0, 1):
-            for i in range(6):
-                tile = turn(messages[0], -(8 * g2 + i))
-                for q in range(1, 16):
-                    tile = jnp.where(granule[q], turn(messages[q], q - 8 * g2 - i), tile)
-                blocks.append(tile)
-            blocks.append(jnp.zeros((16, 128), f32))
-    found = split(jnp.concatenate(blocks, axis=0))
-    lines[...] = dot(jnp.concatenate(found, axis=1), inv[0:256]) + dot(found[0], inv[256:384])
-
-    def synthesise(i, carry):
-        first = pl.multiple_of(i * 8, 8)
-        even, odd = {}, {}
-        for r in range(1, 8):
-            co, si = tw(r)
-            at = pl.ds(64 * place((r - 1) // 2) + first, 8)
-            column = 256 * ((r - 1) % 2)
-            re, im = lines[at, pl.ds(column, 128)], lines[at, pl.ds(column + 128, 128)]
-            even[r] = re * co - im * si
-            odd[r] = re * si + im * co
-        at = pl.ds(192 + first, 8)
-        c, s = sixteen(lines[at, pl.ds(512, 128)], lines[at, pl.ds(640, 128)], even, odd)
-        s6[0, pl.ds(first, 8)] = c[0]
-        s6[8, pl.ds(first, 8)] = c[8]
-        for d in range(1, 8):
-            s6[d, pl.ds(first, 8)] = c[d] - s[d]
-            s6[16 - d, pl.ds(first, 8)] = c[d] + s[d]
-        return carry
-
-    lax.fori_loop(0, ROWS // 8, synthesise, 0)
-    keep = pltpu.make_async_copy(s6.at[p], normal_hbm.at[p], local.at[1])
-    keep.start()
-    exchange("lon", p, LONS, s6, normal_hbm, send_sem.at[5], recv_sem.at[5])
-    for i, (buffer, count) in enumerate([(s1, LONS), (s3, LATS), (s4, LATS), (s6, LONS)]):
-        drain(buffer, count, send_sem.at[(0, 2, 3, 5)[i]])
-    second.wait_send()
-    fifth.wait_send()
+    drain(s1, LONS, send_sem.at[0], 32)
+    drain(s3, LATS, send_sem.at[2])
+    drain(s4, LATS, send_sem.at[3])
+    drain(s6, LONS, send_sem.at[4], 32)
+    for kind, rows, blocks16 in ((four, 32, 11), (three, 16, 12), (two, 0, 13)):
+
+        @pl.when(kind)
+        def _():
+            drain(s1, blocks16 + 1, send_sem.at[1], 16)
+            if rows:
+                drain(s6, LONS, send_sem.at[5], rows)
+            drain(normal_hbm, blocks16 + 1, recv_sem.at[5], 16)
+
     for copy in halos:
         copy.wait_send()
     put_base.wait()
     keep.wait()
-    drain(normal_hbm, LONS, recv_sem.at[5])
-
-
-def finish(base_hbm, circles_hbm, jrad, out_hbm, normal, circles, base, sem):
+    drain(normal_hbm, LONS, recv_sem.at[4], 32)
+
+
+def finish(base_hbm, circles_hbm, jrad, out_hbm, normal_hbm, circles, base, normal, change, sem):
     b = lax.axis_index("lat")
     get_circles = pltpu.make_async_copy(circles_hbm, circles, sem.at[0])
     get_circles.start()
@@ -607,6 +643,10 @@
         copy.start()
     jr = [[jrad[v, w] for w in range(VARS)] for v in range(VARS)]
     row = lax.broadcasted_iota(jnp.int32, (8, 128), 0)
+    puts = [
+        pltpu.make_async_copy(base.at[part(v)], out_hbm.at[part(v)], sem.at[1 + v])
+        for v in range(VARS)
+    ]
     get_circles.wait()
     for h in (0, 1):
         band = (16 * b + 8 * h + row).astype(f32)
@@ -617,8 +657,8 @@
             value = {}
             for k in range(5):
                 for kind in (0, 1) if k else (0,):
-                    z, i = PLACE[v, k, kind]
-                    value[k, kind] = circles[2 * z + h, pl.ds(8 * i, 8)]
+                    p, i = PLACE[v, k, kind]
+                    value[k, kind] = circles[p, pl.ds(16 * i + 8 * h, 8)]
             even = {k: value[k, 0] for k in range(1, 5)}
             odd = {k: value[k, 1] for k in range(1, 5)}
             c, s = fold_time(value[0, 0], even, odd)
@@ -628,23 +668,22 @@
         for v in range(VARS):
             for t in range(INST):
                 normal[v * INST + t, rows] = n[v, t]
+        if h == 1:
+            put_normal = pltpu.make_async_copy(normal, normal_hbm, sem.at[6])
+            put_normal.start()
         for v in range(VARS):
-            if h == 0:
-                gets[v].wait()
             for t in range(INST):
                 total = -n[v, t]
                 for w in range(VARS):
                     total = total + jr[v][w] * n[w, t]
-                at = v * INST + t
-                base[at, 3, rows] = base[at, 3, rows] + half_sine * total
-    puts = [
-        pltpu.make_async_copy(base.at[part(v)], out_hbm.at[part(v)], sem.at[1 + v])
-        for v in range(VARS)
-    ]
-    for copy in puts:
-        copy.start()
+                change[v * INST + t, rows] = half_sine * total
+    for v in range(VARS):
+        gets[v].wait()
+        base[part(v), 3] = base[part(v), 3] + change[part(v)]
+        puts[v].start()
     for copy in puts:
         copy.wait()
+    put_normal.wait()
 
 
 def shards(flow_state, jacobian_lat, jacobian_lon, jacobian_rad, ratio_real, ratio_imag, cut):
@@ -663,7 +702,6 @@
     ]
     constants = [jnp.asarray(part) for part in constants]
     smem = pl.BlockSpec(memory_space=pltpu.SMEM)
-    vmem = pl.BlockSpec(memory_space=pltpu.VMEM)
     hbm = pl.BlockSpec(memory_space=pl.ANY)
     v = lambda *shape: pltpu.VMEM(shape, f32)
     w = lambda *shape: pltpu.VMEM(shape, bf16)
@@ -678,16 +716,14 @@
         scratch_shapes=[
             v(FIELDS, 16, 128), v(FIELDS, RAD, 16, 128), v(FIELDS, RAD, 16, 128),
             v(16, ROWS, 128), v(16, ROWS, 128),
-            v(2, 16, 8, 128), v(2, 16, 8, 128),
             v(32, 8, 128), v(32, 8, 128),
             v(32, 8, 128), v(32, 8, 128),
-            v(2, 16, 8, 128), v(2, 16, 8, 128),
             v(16, ROWS, 128),
             v(2, 180, 128), v(2, 180, 128), v(2, 2, 16, 128), v(2, 2, 16, 128),
-            v(256, 768), v(256, 768), v(4, MODES * 8, 128),
+            v(256, 768), v(256, 768), v(8, MODES * 8, 128),
             w(8, 256, 256), w(8, 256, 256), w(8, 256, 256), w(8, 256, 256),
-            v(4, MODES, 128), v(4, MODES, 128), v(4, MODES, 128), v(2, MODES, 128),
-            w(768, 256), w(384, 768), v(56, 128), v(8, 16, 128),
+            v(8, MODES, 128), v(8, MODES, 128), v(8, MODES, 128), v(3, MODES, 128),
+            w(768, 256), w(384, 768), v(56, 128), v(16, 16, 128),
             pltpu.SMEM((5, 5), f32), pltpu.SMEM((5, 5), f32), pltpu.SMEM((5, 5), f32),
             pltpu.SMEM((5,), jnp.int32), v(5, MODES), v(4, MODES),
             pltpu.SemaphoreType.DMA((6,)), pltpu.SemaphoreType.DMA((6,)),
@@ -707,9 +743,10 @@
             jax.ShapeDtypeStruct((FIELDS, 16, 128), f32),
         ],
         in_specs=[hbm, hbm, smem],
-        out_specs=[hbm, vmem],
+        out_specs=[hbm, hbm],
         scratch_shapes=[
-            v(16, ROWS, 128), v(FIELDS, RAD, 16, 128), pltpu.SemaphoreType.DMA((6,))
+            v(16, ROWS, 128), v(FIELDS, RAD, 16, 128), v(FIELDS, 16, 128),
+            v(FIELDS, 16, 128), pltpu.SemaphoreType.DMA((7,)),
         ],
         compiler_params=pltpu.CompilerParams(vmem_limit_bytes=62 * 1024 * 1024),
         name="finish",

time: 66.6 us -> 60.9 us (0.914)
  Pallas kernels: 65.6 us -> 60 us
    pallas_call x1, Pallas kernels: 61.4 us -> 56.7 us  [shards(): pl.pallas_call(far_field, out_shape=[jax.ShapeDtypeStruct((FIELDS, RAD, 1...]
    pallas_call x1, Pallas kernels: 4.21 us -> 3.3 us  [shards(): pl.pallas_call(finish, out_shape=[jax.ShapeDtypeStruct((FIELDS, RAD, 16,...]
where the time goes in v3:
time: 60.9 us; the launch traced here: 60.7 us
  Pallas kernels  60 us (99%)
  between operations  0.64 us (1%)
    pallas_call x1, Pallas kernels, shards(): pl.pallas_call(far_field, out_shape=[jax.ShapeDtypeStruct((FIELDS, RAD, 1...  56.7 us
    pallas_call x1, Pallas kernels, shards(): pl.pallas_call(finish, out_shape=[jax.ShapeDtypeStruct((FIELDS, RAD, 16,...  3.3 us

profile of v3, /device:TPU:1, one launch (start us, length us, event | category | flops | bytes accessed | tf_op | source)
XLA Modules:
  0.0 60.7 jit_solution(13182018195356497672)
XLA Ops:
  0.6 56.7 %far_field.1 = (f32[45,4,16,128]{3,2,1,0:T(8,128)}, f32[16,64,128]{2,1,0:T(8,128)}) custom-call(f32[45,4,16,128]{3,2,1,0:T(8,128)} %bitcast.5, f32[5,5]{1,0:T(8,128)} %jlat_hbm.1, f32[5,5]{1,0:T(8,128)} %jlon_hbm.1, f32[5,5]{1,0:T(8,128)} %jrad.1, s32[5]{0:T(128)} %cut_hbm.1, f32[5,256]{1,0:T(8,128)} %bitcast.6, f32[4,256]{1,0:T(4,128)} %bitcast.7, ...), custom_call_target="tpu_custom_call" | custom-call | tf_op jit(solution)/shard_map/far_field/pallas_call | solution.py:708
  57.4 3.3 %finish.1 = (f32[45,4,16,128]{3,2,1,0:T(8,128)}, f32[45,16,128]{2,1,0:T(8,128)}) custom-call(f32[45,4,16,128]{3,2,1,0:T(8,128)} %get-tuple-element.6.base_hbm, f32[16,64,128]{2,1,0:T(8,128)} %get-tuple-element.7.circles_hbm, f32[5,5]{1,0:T(8,128)} %jrad.1), custom_call_target="tpu_custom_call" | custom-call | tf_op jit(solution)/shard_map/finish/pallas_call | solution.py:739

commit v4 on v3

--- a/solution.py
+++ b/solution.py
@@ -55,7 +55,7 @@
     return np.concatenate([np.cos(angle), np.sin(angle)])
 
 
-FOUR, THREE = (0, 5, 8, 13), (2, 3, 7, 10, 15)
+FOUR, THREE = (0, 9, 10, 15), (1, 8, 11, 13, 14)
 
 
 def slot_table():
@@ -267,6 +267,7 @@
             s1[d, pl.ds(16 * i, 16)] = value
     r1[p] = s1[p]
     pl.semaphore_wait(barrier, LONS + LATS - 2)
+    exchange("lon", p, LONS, s1, r1, send_sem.at[0], recv_sem.at[0], lower)
     for group, rows in ((FOUR, upper), (THREE, middle)):
         for peer in group:
 
@@ -281,8 +282,6 @@
                     device_id_type=MESH,
                 ).start()
 
-
-    exchange("lon", p, LONS, s1, r1, send_sem.at[0], recv_sem.at[0], lower)
 
     get_all.wait()
     lane = lax.broadcasted_iota(jnp.int32, (16, 128), 1)
@@ -418,10 +417,100 @@
     weight = (2.0 / NLAT) * (1.0 - 2.0 * series) * (2.0 * math.pi / NLON)
     weight = jnp.broadcast_to(weight, (16, 128))
 
-    circles[pl.ds(0, 192), pl.ds(512, 256)] = jnp.zeros((192, 256), f32)
-    circles[pl.ds(192, 64), pl.ds(256, 256)] = jnp.zeros((64, 256), f32)
+    for k in (0, 1):
+        circles[k, pl.ds(0, 96), pl.ds(512, 256)] = jnp.zeros((96, 256), f32)
+        circles[k, pl.ds(96, 32), pl.ds(256, 256)] = jnp.zeros((32, 256), f32)
     tw = lambda r: (small[16 + r : 17 + r], small[24 + r : 25 + r])
+    several = jnp.logical_not(two)
+    lane8 = lax.broadcasted_iota(jnp.int32, (8, 128), 1)
+    granule = [lane8 // 8 == i for i in range(16)]
+
+    def turn(value, granules):
+        return pltpu.roll(value, (8 * granules) % 128, 1) if granules % 16 else value
+
+    def forward(k):
+        def analyse(i, carry):
+            first = pl.multiple_of(i * 8, 8)
+            x = [r1[d, pl.ds(32 * k + first, 8)] for d in range(16)]
+            even = {d: x[d] + x[16 - d] for d in range(1, 8)}
+            odd = {d: x[d] - x[16 - d] for d in range(1, 8)}
+            c, s = sixteen(x[0], x[8], even, odd)
+            for r in range(1, 8):
+                co, si = tw(r)
+                at = pl.ds(32 * ((r - 1) // 2) + first, 8)
+                column = 256 * ((r - 1) % 2)
+                circles[k, at, pl.ds(column, 128)] = c[r] * co - s[r] * si
+                circles[k, at, pl.ds(column + 128, 128)] = -s[r] * co - c[r] * si
+            at = pl.ds(96 + first, 8)
+            circles[k, at, pl.ds(512, 128)] = c[0]
+            circles[k, at, pl.ds(640, 128)] = c[8]
+            return carry
+
+        lax.fori_loop(0, 4, analyse, 0)
+        found = dot_wide(split(circles[k]), fwd[...])
+        for side in (0, 1):
+            tiles = {}
+            for h in (0, 1):
+                for i in (0, 1):
+                    for low in (0, 1):
+                        first = 32 * (2 * side + low) + 16 * i + 8 * h
+                        tile = found[first : first + 8] * weight[8 * h : 8 * h + 8]
+                        tiles[8 * h + 2 * (2 * k + i) + low] = tile
+            for q in range(16):
+                to = 2 * q + side
+                message = s3[to] if k else jnp.zeros((8, 128), f32)
+                for i, tile in tiles.items():
+                    message = jnp.where(granule[i], turn(tile, i - q), message)
+                s3[to] = message
+
+    def keep(k):
+        rows = pl.ds(32 * k, 32)
+        return pltpu.make_async_copy(s6.at[p, rows], normal_hbm.at[p, rows], local.at[2 + k])
+
+    def backward(k):
+        blocks = []
+        for g in range(4):
+            messages = [r4[2 * q + g // 2] for q in range(16)]
+            for i in (0, 1):
+                for h in (0, 1):
+                    at = 8 * h + 2 * (2 * k + i) + g % 2
+                    tile = turn(messages[0], -at)
+                    for q in range(1, 16):
+                        tile = jnp.where(granule[q], turn(messages[q], q - at), tile)
+                    blocks.append(tile)
+        found = split(jnp.concatenate(blocks, axis=0))
+        lines[k] = dot(jnp.concatenate(found, axis=1), inv[0:256]) + dot(found[0], inv[256:384])
+
+        def synthesise(i, carry):
+            first = pl.multiple_of(i * 8, 8)
+            even, odd = {}, {}
+            for r in range(1, 8):
+                co, si = tw(r)
+                at = pl.ds(32 * ((r - 1) // 2) + first, 8)
+                column = 256 * ((r - 1) % 2)
+                re, im = lines[k, at, pl.ds(column, 128)], lines[k, at, pl.ds(column + 128, 128)]
+                even[r] = re * co - im * si
+                odd[r] = re * si + im * co
+            at = pl.ds(96 + first, 8)
+            c, s = sixteen(lines[k, at, pl.ds(512, 128)], lines[k, at, pl.ds(640, 128)], even, odd)
+            to = pl.ds(32 * k + first, 8)
+            s6[0, to] = c[0]
+            s6[8, to] = c[8]
+            for d in range(1, 8):
+                s6[d, to] = c[d] - s[d]
+                s6[16 - d, to] = c[d] + s[d]
+            return carry
+
+        lax.fori_loop(0, 4, synthesise, 0)
+        keep(k).start()
+
+    def send_circles(k, rows):
+        exchange(
+            "lon", p, LONS, s6, normal_hbm, send_sem.at[6 + k], recv_sem.at[6 + k], rows
+        )
+
     drain(r1, LONS, recv_sem.at[0], 32)
+    forward(0)
 
     @pl.when(four)
     def _():
@@ -431,45 +520,10 @@
     def _():
         drain(r1, LONS, recv_sem.at[1], 16)
 
-
-    def analyse(i, carry):
-        first = pl.multiple_of(i * 8, 8)
-        x = [r1[d, pl.ds(first, 8)] for d in range(16)]
-        even = {d: x[d] + x[16 - d] for d in range(1, 8)}
-        odd = {d: x[d] - x[16 - d] for d in range(1, 8)}
-        c, s = sixteen(x[0], x[8], even, odd)
-        for r in range(1, 8):
-            co, si = tw(r)
-            at = pl.ds(64 * ((r - 1) // 2) + first, 8)
-            column = 256 * ((r - 1) % 2)
-            circles[at, pl.ds(column, 128)] = c[r] * co - s[r] * si
-            circles[at, pl.ds(column + 128, 128)] = -s[r] * co - c[r] * si
-        at = pl.ds(192 + first, 8)
-        circles[at, pl.ds(512, 128)] = c[0]
-        circles[at, pl.ds(640, 128)] = c[8]
-        return carry
-
-    lax.fori_loop(0, ROWS // 8, analyse, 0)
-    found = dot_wide(split(circles[...]), fwd[...])
-    lane8 = lax.broadcasted_iota(jnp.int32, (8, 128), 1)
-    low_half = lane8 < 64
-    granule = [lane8 // 8 == i for i in range(16)]
-
-    def turn(value, granules):
-        return pltpu.roll(value, (8 * granules) % 128, 1) if granules % 16 else value
-
-    for side in (0, 1):
-        tiles = []
-        for h in (0, 1):
-            for i in range(4):
-                for low in (0, 1):
-                    first = 64 * (2 * side + low) + 16 * i + 8 * h
-                    tiles.append(found[first : first + 8] * weight[8 * h : 8 * h + 8])
-        for q in range(16):
-            message = turn(tiles[0], -q)
-            for i in range(1, 16):
-                message = jnp.where(granule[i], turn(tiles[i], i - q), message)
-            s3[2 * q + side] = message
+    @pl.when(several)
+    def _():
+        forward(1)
+
     r3[b] = s3[b]
     exchange("lat", b, LATS, s3, r3, send_sem.at[2], recv_sem.at[2])
     def pack(f, packed):
@@ -491,6 +545,7 @@
 
     drain(r3, LATS, recv_sem.at[2])
 
+    low_half = lane8 < 64
     folded = [jnp.where(low_half, r3[i], mirrored(r3[LATS - 1 - i])) for i in range(LATS)]
     wide = jnp.concatenate(split(jnp.concatenate(folded, axis=0)), axis=1)
     degrees = jnp.zeros((MODES, 128), f32)
@@ -513,51 +568,21 @@
     exchange("lat", b, LATS, s4, r4, send_sem.at[3], recv_sem.at[3])
     drain(r4, LATS, recv_sem.at[3])
 
-    blocks = []
-    for g in range(4):
-        messages = [r4[2 * q + g // 2] for q in range(16)]
-        for i in range(4):
-            for h in (0, 1):
-                at = 8 * h + 2 * i + g % 2
-                tile = turn(messages[0], -at)
-                for q in range(1, 16):
-                    tile = jnp.where(granule[q], turn(messages[q], q - at), tile)
-                blocks.append(tile)
-    found = split(jnp.concatenate(blocks, axis=0))
-    lines[...] = dot(jnp.concatenate(found, axis=1), inv[0:256]) + dot(found[0], inv[256:384])
-
-    def synthesise(i, carry):
-        first = pl.multiple_of(i * 8, 8)
-        even, odd = {}, {}
-        for r in range(1, 8):
-            co, si = tw(r)
-            at = pl.ds(64 * ((r - 1) // 2) + first, 8)
-            column = 256 * ((r - 1) % 2)
-            re, im = lines[at, pl.ds(column, 128)], lines[at, pl.ds(column + 128, 128)]
-            even[r] = re * co - im * si
-            odd[r] = re * si + im * co
-        at = pl.ds(192 + first, 8)
-        c, s = sixteen(lines[at, pl.ds(512, 128)], lines[at, pl.ds(640, 128)], even, odd)
-        s6[0, pl.ds(first, 8)] = c[0]
-        s6[8, pl.ds(first, 8)] = c[8]
-        for d in range(1, 8):
-            s6[d, pl.ds(first, 8)] = c[d] - s[d]
-            s6[16 - d, pl.ds(first, 8)] = c[d] + s[d]
-        return carry
-
-    lax.fori_loop(0, ROWS // 8, synthesise, 0)
-    keep = pltpu.make_async_copy(s6.at[p], normal_hbm.at[p], local.at[1])
-    keep.start()
-    parts = ((four, upper), (three, middle), (None, lower))
-    for kind, rows in parts:
-        send = lambda: exchange(
-            "lon", p, LONS, s6, normal_hbm,
-            send_sem.at[4 if kind is None else 5], recv_sem.at[4 if kind is None else 5], rows,
-        )
-        if kind is None:
-            send()
-        else:
-            pl.when(kind)(send)
+    backward(0)
+    send_circles(0, lower)
+
+    @pl.when(several)
+    def _():
+        backward(1)
+
+    @pl.when(four)
+    def _():
+        send_circles(1, upper)
+
+    @pl.when(three)
+    def _():
+        send_circles(1, middle)
+
     for i in (2, 3, 0, 1):
         halos[i].wait_recv()
     band = (16 * b + row).astype(f32)
@@ -613,21 +638,22 @@
     drain(s1, LONS, send_sem.at[0], 32)
     drain(s3, LATS, send_sem.at[2])
     drain(s4, LATS, send_sem.at[3])
-    drain(s6, LONS, send_sem.at[4], 32)
+    drain(s6, LONS, send_sem.at[6], 32)
+    keep(0).wait()
     for kind, rows, blocks16 in ((four, 32, 11), (three, 16, 12), (two, 0, 13)):
 
         @pl.when(kind)
         def _():
             drain(s1, blocks16 + 1, send_sem.at[1], 16)
             if rows:
-                drain(s6, LONS, send_sem.at[5], rows)
-            drain(normal_hbm, blocks16 + 1, recv_sem.at[5], 16)
+                drain(s6, LONS, send_sem.at[7], rows)
+                keep(1).wait()
+            drain(normal_hbm, blocks16 + 1, recv_sem.at[7], 16)
 
     for copy in halos:
         copy.wait_send()
     put_base.wait()
-    keep.wait()
-    drain(normal_hbm, LONS, recv_sem.at[4], 32)
+    drain(normal_hbm, LONS, recv_sem.at[6], 32)
 
 
 def finish(base_hbm, circles_hbm, jrad, out_hbm, normal_hbm, circles, base, normal, change, sem):
@@ -720,13 +746,13 @@
             v(32, 8, 128), v(32, 8, 128),
             v(16, ROWS, 128),
             v(2, 180, 128), v(2, 180, 128), v(2, 2, 16, 128), v(2, 2, 16, 128),
-            v(256, 768), v(256, 768), v(8, MODES * 8, 128),
+            v(2, 128, 768), v(2, 128, 768), v(8, MODES * 8, 128),
             w(8, 256, 256), w(8, 256, 256), w(8, 256, 256), w(8, 256, 256),
             v(8, MODES, 128), v(8, MODES, 128), v(8, MODES, 128), v(3, MODES, 128),
             w(768, 256), w(384, 768), v(56, 128), v(16, 16, 128),
             pltpu.SMEM((5, 5), f32), pltpu.SMEM((5, 5), f32), pltpu.SMEM((5, 5), f32),
             pltpu.SMEM((5,), jnp.int32), v(5, MODES), v(4, MODES),
-            pltpu.SemaphoreType.DMA((6,)), pltpu.SemaphoreType.DMA((6,)),
+            pltpu.SemaphoreType.DMA((8,)), pltpu.SemaphoreType.DMA((8,)),
             pltpu.SemaphoreType.DMA((4,)), pltpu.SemaphoreType.DMA((4,)),
             pltpu.SemaphoreType.DMA((12,)),
         ],

time: 60.9 us -> 59.8 us (0.982)
  Pallas kernels: 60 us -> 58.8 us
    pallas_call x1, Pallas kernels: 56.7 us -> 55.5 us  [shards(): pl.pallas_call(far_field, out_shape=[jax.ShapeDtypeStruct((FIELDS, RAD, 1...]
where the time goes in v4:
time: 59.8 us; the launch traced here: 59.5 us
  Pallas kernels  58.8 us (98%)
  between operations  0.64 us (1%)
    pallas_call x1, Pallas kernels, shards(): pl.pallas_call(far_field, out_shape=[jax.ShapeDtypeStruct((FIELDS, RAD, 1...  55.5 us
    pallas_call x1, Pallas kernels, shards(): pl.pallas_call(finish, out_shape=[jax.ShapeDtypeStruct((FIELDS, RAD, 16,...  3.3 us

profile of v4, /device:TPU:1, one launch (start us, length us, event | category | flops | bytes accessed | tf_op | source)
XLA Modules:
  0.0 59.5 jit_solution(18382057346862718922)
XLA Ops:
  0.6 55.5 %far_field.1 = (f32[45,4,16,128]{3,2,1,0:T(8,128)}, f32[16,64,128]{2,1,0:T(8,128)}) custom-call(f32[45,4,16,128]{3,2,1,0:T(8,128)} %bitcast.5, f32[5,5]{1,0:T(8,128)} %jlat_hbm.1, f32[5,5]{1,0:T(8,128)} %jlon_hbm.1, f32[5,5]{1,0:T(8,128)} %jrad.1, s32[5]{0:T(128)} %cut_hbm.1, f32[5,256]{1,0:T(8,128)} %bitcast.6, f32[4,256]{1,0:T(4,128)} %bitcast.7, ...), custom_call_target="tpu_custom_call" | custom-call | tf_op jit(solution)/shard_map/far_field/pallas_call | solution.py:734
  56.2 3.3 %finish.1 = (f32[45,4,16,128]{3,2,1,0:T(8,128)}, f32[45,16,128]{2,1,0:T(8,128)}) custom-call(f32[45,4,16,128]{3,2,1,0:T(8,128)} %get-tuple-element.6.base_hbm, f32[16,64,128]{2,1,0:T(8,128)} %get-tuple-element.7.circles_hbm, f32[5,5]{1,0:T(8,128)} %jrad.1), custom_call_target="tpu_custom_call" | custom-call | tf_op jit(solution)/shard_map/finish/pallas_call | solution.py:765
